TPU v7x, 256 devices: a whole 4x4x8 slice. The times are simulated.
256 devices in a mesh: dp: 64 (over z, x, core), mp: 4 (over y).
Axes of the slice: x: 4, y: 4, z: 8, core: 2. Of those that a mesh axis runs over, the one named last changes fastest.
Arguments:
- grad_parts: float32 [64, 2048, 2048], P('dp', None, 'mp'), may hold values from -16 to 16
- master: float32 [2048, 2048], P('dp', 'mp'), may hold values from -0.125 to 0.125
- moment_one: float32 [2048, 2048], P('dp', 'mp'), may hold values from -6 to 6
- moment_two: float32 [2048, 2048], P('dp', 'mp'), may hold values from 0.02 to 0.16
- states: bfloat16 [32768, 2048], P('dp'), may hold values from -6 to 6
- action_ids: int32 [32768, 4], P('dp'), may hold values from 0 to 255
- env_counts: int32 [64], P('dp'), may hold values from 256 to 512, as said below
- owners: int32 [32768, 1], P('dp'), may hold values from 0 to 63; in each aligned block of 512 rows (0 to 511, 512 to 1023, ...) at most 12 rows name the same one
- act_table: bfloat16 [256, 2048], replicated, may hold values from -6 to 6
- norm_gain: float32 [2048], replicated, may hold values from 0.1 to 1.9
- head: bfloat16 [2048, 256], P(None, 'mp'), may hold values from -0.125 to 0.125
Outputs:
- moment_one_new: float32 [2048, 2048], P('dp', 'mp')
- moment_two_new: float32 [2048, 2048], P('dp', 'mp')
- master_new: float32 [2048, 2048], P('dp', 'mp')
- logits: float32 [32768, 256], P('dp', 'mp')
- received: bfloat16 [49152, 2048], P('dp', 'mp')
Inputs may be any that keep to these rules, and one draw needn't show every extreme that they name: `env_counts`: every actor has at least half of its slots live, and some actor has all 512 live. `owners`: among the rows of one actor at most 12 name the same owner, and some actor's rows reach 12 for some owner.
All inputs are finite; a program needn't handle non-finite values.
Results may differ from a plain program's by a relative error of at most 0.017.
Values may be sent and summed in bfloat16 or wider, within the bound.
No kernel may reach another device: no remote copies, remote signals or barrier semaphores. Data moves between devices by JAX's collectives and lax.ppermute only.
A program may use at most 64 MiB of HBM per device.

v0:
```python
import jax
import jax.numpy as jnp
from jax import lax
from jax.sharding import PartitionSpec as P

STEPS = 4


beta_one = 0.9
beta_two = 0.999
corr_one = 1.0 - 0.9**10
corr_two = 1.0 - 0.999**10
rate_lr = 0.01
adam_eps = 1e-08
norm_eps = 1e-06


def body(
    grad_parts,
    master,
    moment_one,
    moment_two,
    states,
    action_ids,
    env_counts,
    owners,
    act_table,
    norm_gain,
    head,
):
    gradient = lax.psum_scatter(grad_parts[0], "dp", scatter_dimension=0, tiled=True)
    m_new = beta_one * moment_one + (1.0 - beta_one) * gradient
    v_new = beta_two * moment_two + (1.0 - beta_two) * gradient * gradient
    w_new = master - rate_lr * (m_new / corr_one) / (jnp.sqrt(v_new / corr_two) + adam_eps)
    weights = lax.all_gather(w_new.astype(jnp.bfloat16), "dp", axis=0, tiled=True)
    env_slots = states.shape[0]
    width_cols = weights.shape[1]
    actions_num = act_table.shape[0]
    col_start = lax.axis_index("mp") * width_cols
    active = jnp.arange(env_slots, dtype=jnp.int32) < env_counts[0]
    action_iota = jnp.arange(actions_num, dtype=jnp.int32)
    state = states
    for step_idx in range(STEPS):
        onehot = (action_ids[:, step_idx][:, None] == action_iota[None, :]).astype(jnp.bfloat16)
        embedded = jnp.dot(onehot, act_table, preferred_element_type=jnp.float32)
        hidden = (state.astype(jnp.float32) + embedded).astype(jnp.bfloat16)
        mixed = jnp.dot(hidden, weights, preferred_element_type=jnp.float32).astype(jnp.bfloat16)
        gathered = lax.all_gather(mixed, "mp", axis=1, tiled=True)
        mixed_f = gathered.astype(jnp.float32)
        inverse = lax.rsqrt(jnp.mean(mixed_f * mixed_f, axis=1) + norm_eps)
        state = (
            state.astype(jnp.float32) + norm_gain[None, :] * mixed_f * inverse[:, None]
        ).astype(jnp.bfloat16)
    scores = jnp.dot(state, head, preferred_element_type=jnp.float32)
    logits = scores * active[:, None].astype(jnp.float32)
    owner_num = lax.axis_size("dp")
    capacity = max(2, 3 * env_slots // (2 * owner_num))
    target = owners[:, 0]
    marks = (
        (target[:, None] == jnp.arange(owner_num, dtype=jnp.int32)[None, :]) & active[:, None]
    ).astype(jnp.int32)
    ranked = jnp.cumsum(marks, axis=0) - marks
    slot_idx = jnp.sum(ranked * marks, axis=1)
    index = jnp.where(active, target * capacity + slot_idx, owner_num * capacity)
    own_cols = lax.dynamic_slice_in_dim(state, col_start, width_cols, 1)
    buffer = (
        jnp.zeros((owner_num * capacity, width_cols), jnp.bfloat16)
        .at[index]
        .set(own_cols, mode="drop")
    )
    arrived = lax.all_to_all(
        buffer.reshape(owner_num, capacity, width_cols),
        "dp",
        split_axis=0,
        concat_axis=0,
        tiled=True,
    )
    received = arrived.reshape(owner_num * capacity, width_cols)
    return (m_new, v_new, w_new, logits, received)


def solution(mesh):
    in_specs = (
        P("dp", None, "mp"),
        P("dp", "mp"),
        P("dp", "mp"),
        P("dp", "mp"),
        P("dp", None),
        P("dp", None),
        P("dp"),
        P("dp", None),
        P(),
        P(),
        P(None, "mp"),
    )
    out_specs = (P("dp", "mp"), P("dp", "mp"), P("dp", "mp"), P("dp", "mp"), P("dp", "mp"))
    return jax.shard_map(body, mesh=mesh, in_specs=in_specs, out_specs=out_specs, check_vma=False)
```

profile of v0, /device:TPU:1, one launch (start us, length us, event | category | flops | bytes accessed | tf_op | source)
XLA Modules:
  0.0 460.6 jit_solution(1019336268006325582)
XLA Ops:
  7.3 0.7 reduce-scatter.2.cloned.1.call-update
  8.0 0.0 all-gather.6.cloned.1.call-start
  8.0 146.8 %reduce-scatter.2.cloned.1.call-done = f32[32,512]{1,0:T(8,128)} async-done(((f32[2048,512]{1,0:T(8,128)}), f32[32,512]{1,0:T(8,128)}) %reduce-scatter.2.cloned.1.call-update) | async-done | bytes 65552 | tf_op jit(solution)/shard_map/reduce_scatter | solution.py:31
  154.8 1.5 fusion.37
  156.4 0.0 all-gather.8.cloned.1.call-start
  156.5 83.1 %all-gather.6.cloned.1.call-done = bf16[2048,512]{1,0:T(8,128)(2,1)} async-done(((bf16[32,512]{1,0:T(8,128)(2,1)}), bf16[2048,512]{1,0:T(8,128)(2,1)}) %all-gather.6.cloned.1.call-update) | async-done | bytes 2097168 | tf_op jit(solution)/shard_map/all_gather | solution.py:35
  239.5 4.2 convolution_convert_fusion.3
  243.8 0.0 all-gather.10.cloned.1.call-start
  243.9 30.8 %all-gather.8.cloned.1.call-done = bf16[512,2048]{1,0:T(8,128)(2,1)} async-done(((bf16[512,512]{1,0:T(8,128)(2,1)}), bf16[512,2048]{1,0:T(8,128)(2,1)}) %all-gather.8.cloned.1.call-update) | async-done | bytes 2097168 | tf_op jit(solution)/shard_map/all_gather | solution.py:48
  274.7 2.1 fusion.3
  276.8 5.0 %convolution_convert_fusion.2 = bf16[512,512]{1,0:T(8,128)(2,1)} fusion(bf16[2048,512]{1,0:T(8,128)(2,1)} %all-gather.6.cloned.1.call-done, bf16[256,2048]{1,0:T(8,128)(2,1)S(1)} %copy-done, s32[512]{0:T(512)S(1)} %bitcast.50, bf16[512,2048]{1,0:T(8,128)(2,1)S(1)} %copy-done.2, bf16[512,2048]{1,0:T(8,128)(2,1)} %all-gather.8.cloned.1.call-done, ...), kind=kOutput, calls=%fused_computation.35 | convolution fusion | flops 1620443136 | bytes 7876608 | tf_op jit(solution)/shard_map/dot_general | solution.py:47
  281.8 0.0 all-gather.12.cloned.1.call-start
  281.9 33.5 %all-gather.10.cloned.1.call-done = bf16[512,2048]{1,0:T(8,128)(2,1)} async-done(((bf16[512,512]{1,0:T(8,128)(2,1)}), bf16[512,2048]{1,0:T(8,128)(2,1)}) %all-gather.10.cloned.1.call-update) | async-done | bytes 2097168 | tf_op jit(solution)/shard_map/all_gather | solution.py:48
  315.4 2.1 fusion.7
  317.5 4.2 fusion.5
  321.7 5.0 %convolution_convert_fusion.1 = bf16[512,512]{1,0:T(8,128)(2,1)} fusion(bf16[2048,512]{1,0:T(8,128)(2,1)} %all-gather.6.cloned.1.call-done, bf16[512,2048]{1,0:T(8,128)(2,1)S(1)} %fusion.5, bf16[256,2048]{1,0:T(8,128)(2,1)S(1)} %copy-done, s32[512]{0:T(512)S(1)} %bitcast.49), kind=kOutput, calls=%fused_computation.34 | convolution fusion | flops 1614151680 | bytes 5769216 | tf_op jit(solution)/shard_map/dot_general | solution.py:47
  326.7 0.2 all-gather.14.cloned.1.call-start
  327.0 33.4 %all-gather.12.cloned.1.call-done = bf16[512,2048]{1,0:T(8,128)(2,1)} async-done(((bf16[512,512]{1,0:T(8,128)(2,1)}), bf16[512,2048]{1,0:T(8,128)(2,1)}) %all-gather.12.cloned.1.call-update) | async-done | bytes 2097168 | tf_op jit(solution)/shard_map/all_gather | solution.py:48
  360.3 2.1 fusion.11
  362.4 5.0 %convolution_convert_fusion = bf16[512,512]{1,0:T(8,128)(2,1)} fusion(bf16[2048,512]{1,0:T(8,128)(2,1)} %all-gather.6.cloned.1.call-done, bf16[256,2048]{1,0:T(8,128)(2,1)S(1)} %copy-done, s32[512]{0:T(512)S(1)} %bitcast.48, bf16[512,2048]{1,0:T(8,128)(2,1)S(1)} %fusion.5, bf16[512,2048]{1,0:T(8,128)(2,1)} %all-gather.12.cloned.1.call-done, ...), kind=kOutput, calls=%fused_computation.33 | convolution fusion | flops 1620443136 | bytes 7876608 | tf_op jit(solution)/shard_map/dot_general | solution.py:47
  368.2 1.2 reduce-window.6
  369.4 0.2 slice_reduce_fusion
  369.7 0.1 fusion.29
  369.8 31.3 %all-gather.14.cloned.1.call-done = bf16[512,2048]{1,0:T(8,128)(2,1)} async-done(((bf16[512,512]{1,0:T(8,128)(2,1)}), bf16[512,2048]{1,0:T(8,128)(2,1)}) %all-gather.14.cloned.1.call-update) | async-done | bytes 2097168 | tf_op jit(solution)/shard_map/all_gather | solution.py:48
  401.1 2.1 fusion.15
  403.2 4.2 fusion.13
  407.4 3.3 scatter_custom_fusion
  410.7 2.1 reshape.74
  412.9 10.8 %all-to-all-start = ((bf16[64,12,512]{2,1,0:T(8,128)(2,1)}), bf16[64,12,512]{2,1,0:T(8,128)(2,1)}, u32[]{:S(2)}, u32[]{:S(2)}) async-start(bf16[64,12,512]{2,1,0:T(8,128)(2,1)} %reshape.74), calls=%async_computation.1 | async-start | bytes 2097152 | tf_op jit(solution)/shard_map/all_to_all | solution.py:71
  423.8 1.4 convolution_multiply_fusion
  425.2 26.5 %all-to-all-done = bf16[64,12,512]{2,1,0:T(8,128)(2,1)} async-done(((bf16[64,12,512]{2,1,0:T(8,128)(2,1)}), bf16[64,12,512]{2,1,0:T(8,128)(2,1)}, u32[]{:S(2)}, u32[]{:S(2)}) %all-to-all-start) | async-done | bytes 786464 | tf_op jit(solution)/shard_map/all_to_all | solution.py:71
  451.6 2.1 reshape.75
  (38 shorter events, 0.3 us)
Async XLA Ops:
  7.2 232.4 %copy-start = (bf16[256,2048]{1,0:T(8,128)(2,1)S(1)}, bf16[256,2048]{1,0:T(8,128)(2,1)}, u32[]{:S(2)}) copy-start(bf16[256,2048]{1,0:T(8,128)(2,1)} %param.19) | copy-start | bytes 3145732
  7.2 147.6 %copy-start.4 = (f32[32,512]{1,0:T(8,128)S(1)}, f32[32,512]{1,0:T(8,128)}, u32[]{:S(2)}) copy-start(f32[32,512]{1,0:T(8,128)} %param.12) | copy-start | bytes 196612
  7.2 147.6 %copy-start.5 = (f32[32,512]{1,0:T(8,128)S(1)}, f32[32,512]{1,0:T(8,128)}, u32[]{:S(2)}) copy-start(f32[32,512]{1,0:T(8,128)} %param.14) | copy-start | bytes 196612
  7.2 147.6 %copy-start.6 = (f32[32,512]{1,0:T(8,128)S(1)}, f32[32,512]{1,0:T(8,128)}, u32[]{:S(2)}) copy-start(f32[32,512]{1,0:T(8,128)} %param.13) | copy-start | bytes 196612
  7.2 149.2 %copy-start.9 = (s32[512,4]{0,1:T(4,128)S(1)}, s32[512,4]{0,1:T(4,128)}, u32[]{:S(2)}) copy-start(s32[512,4]{0,1:T(4,128)} %param.16) | copy-start | bytes 24580
  7.2 232.3 %copy-start.2 = (bf16[512,2048]{1,0:T(8,128)(2,1)S(1)}, bf16[512,2048]{1,0:T(8,128)(2,1)}, u32[]{:S(2)}) copy-start(bf16[512,2048]{1,0:T(8,128)(2,1)} %param.15) | copy-start | bytes 6291460
  7.2 147.6 %reduce-scatter.2.cloned.1.call-start = ((), (), s32[]{:S(2)}) async-start(), calls=%async_computation.2 | async-start | bytes 4259840 | tf_op jit(solution)/shard_map/reduce_scatter | solution.py:31
  8.0 231.6 %all-gather.6.cloned.1.call-start = ((), (), s32[]{:S(2)}) async-start(), calls=%async_computation.3 | async-start | bytes 2129920 | tf_op jit(solution)/shard_map/all_gather | solution.py:35
  156.4 118.3 %all-gather.8.cloned.1.call-start = ((), (), s32[]{:S(2)}) async-start(), calls=%async_computation.4 | async-start | bytes 2621440 | tf_op jit(solution)/shard_map/all_gather | solution.py:48
  239.5 37.2 %copy-start.7 = (f32[2048]{0:T(1024)S(1)}, f32[2048]{0:T(1024)}, u32[]{:S(2)}) copy-start(f32[2048]{0:T(1024)} %param.20) | copy-start | bytes 24580
  243.8 71.6 %all-gather.10.cloned.1.call-start = ((), (), s32[]{:S(2)}) async-start(), calls=%async_computation.5 | async-start | bytes 2621440 | tf_op jit(solution)/shard_map/all_gather | solution.py:48
  281.8 78.5 %all-gather.12.cloned.1.call-start = ((), (), s32[]{:S(2)}) async-start(), calls=%async_computation.6 | async-start | bytes 2621440 | tf_op jit(solution)/shard_map/all_gather | solution.py:48
  321.7 40.7 %copy-start.1 = (bf16[512,2048]{1,0:T(8,128)(2,1)}, bf16[512,2048]{1,0:T(8,128)(2,1)S(1)}, u32[]{:S(2)}) copy-start(bf16[512,2048]{1,0:T(8,128)(2,1)S(1)} %fusion.5) | copy-start | bytes 6291460
  326.7 74.4 %all-gather.14.cloned.1.call-start = ((), (), s32[]{:S(2)}) async-start(), calls=%async_computation.7 | async-start | bytes 2621440 | tf_op jit(solution)/shard_map/all_gather | solution.py:48
  362.4 5.8 %copy-start.8 = (s32[512,1]{0,1:T(1,128)S(1)}, s32[512,1]{0,1:T(1,128)}, u32[]{:S(2)}) copy-start(s32[512,1]{0,1:T(1,128)} %param.18) | copy-start | bytes 6148
  407.4 16.4 %copy-start.3 = (bf16[2048,64]{0,1:T(8,128)(2,1)S(1)}, bf16[2048,64]{0,1:T(8,128)(2,1)}, u32[]{:S(2)}) copy-start(bf16[2048,64]{0,1:T(8,128)(2,1)} %param.21) | copy-start | bytes 786436
  412.9 38.8 %all-to-all-start = ((bf16[64,12,512]{2,1,0:T(8,128)(2,1)}), bf16[64,12,512]{2,1,0:T(8,128)(2,1)}, u32[]{:S(2)}, u32[]{:S(2)}) async-start(bf16[64,12,512]{2,1,0:T(8,128)(2,1)} %reshape.74), calls=%async_computation.1 | async-start | bytes 2097152 | tf_op jit(solution)/shard_map/all_to_all | solution.py:71
Sparse Core Ops, SparseCore 0:
  12.2 142.5 reduce-scatter.1
  158.5 80.9 all-gather.5
  243.9 30.7 all-gather.7
  282.0 33.4 all-gather.9
  326.9 33.4 all-gather.11
  367.6 33.4 all-gather.13
where the time goes:
time: 461 us
  waiting for transfers between devices  386 us (84%)
  matrix products  20.7 us (4%)
  other arithmetic  19.7 us (4%)
  between operations  14.9 us (3%)
  starting transfers between devices  11.3 us (2%)
  local copies, waits for them, and re-layouts  7.83 us (2%)
    reduce_scatter x1, waiting for transfers between devices, body(): lax.psum_scatter(grad_parts[0], 'dp', scatter_dimension=0, tiled=True)  147 us
    all_gather x4, waiting for transfers between devices, body(): gathered = lax.all_gather(mixed, 'mp', axis=1, tiled=True)  129 us
    all_gather x1, waiting for transfers between devices, body(): lax.all_gather(w_new.astype(jnp.bfloat16), 'dp', axis=0, tiled=True)  83.1 us
    all_to_all x1, waiting for transfers between devices, body(): lax.all_to_all(buffer.reshape(owner_num, capacity, width_cols), 'dp', spl...  26.5 us
    dot_general x4, matrix products, body(): jnp.dot(hidden, weights, preferred_element_type=jnp.float32)  19.3 us
    all_to_all x1, starting transfers between devices, body(): lax.all_to_all(buffer.reshape(owner_num, capacity, width_cols), 'dp', spl...  10.8 us
  transfers between devices with their start and end apart: 7, of which 7 were waited for; matrix products, arithmetic and copies ran while one was open for 1% of the time, Pallas kernels for 0%

commit v1 on v0

v1 whole, which is shorter than its diff:
```python
import jax
import jax.numpy as jnp
from jax import lax
from jax.sharding import Mesh, PartitionSpec as P

STEPS = 4
NZ, NX, NC, NY = 8, 4, 2, 4
DP = ("z", "x", "c")

beta_one = 0.9
beta_two = 0.999
corr_one = 1.0 - 0.9**10
corr_two = 1.0 - 0.999**10
rate_lr = 0.01
adam_eps = 1e-08
norm_eps = 1e-06
F32 = jnp.float32
BF16 = jnp.bfloat16


def exchange(v, axis):
    return lax.all_to_all(v, axis, 0, 0, tiled=True)


def spread(v, axis, n):
    return exchange(jnp.broadcast_to(v[None], (n,) + v.shape), axis)


def swap(v):
    return lax.ppermute(v, "c", [(0, 1), (1, 0)])


def reduce_part(g):
    me = lax.axis_index("c")
    give = lax.dynamic_index_in_dim(g, 1 - me, 2, keepdims=False).astype(BF16)
    keep = lax.dynamic_index_in_dim(g, me, 2, keepdims=False)
    both = (keep + swap(give).astype(F32)).astype(BF16)
    both = jnp.transpose(both, (1, 0, 2, 3))
    by_x = exchange(both, "x").astype(F32).sum(0).astype(BF16)
    return exchange(by_x, "z").astype(F32).sum(0)


def body(
    grad_parts,
    master,
    moment_one,
    moment_two,
    states,
    action_ids,
    env_counts,
    owners,
    act_table,
    norm_gain,
    head,
):
    width, cols = grad_parts.shape[1:]
    rows = width // (NZ * NX * NC)
    half = cols // 2
    env_slots = states.shape[0]
    actions_num = act_table.shape[0]
    owner_num = NZ * NX * NC
    capacity = max(2, 3 * env_slots // (2 * owner_num))
    share = capacity // NY
    my_y = lax.axis_index("y")

    active = jnp.arange(env_slots, dtype=jnp.int32) < env_counts[0]
    target = owners[:, 0]
    marks = (
        (target[:, None] == jnp.arange(owner_num, dtype=jnp.int32)[None, :]) & active[:, None]
    ).astype(jnp.int32)
    ranked = jnp.cumsum(marks, axis=0) - marks
    slot_idx = jnp.sum(ranked * marks, axis=1)
    mine = active & (slot_idx // share == my_y)
    place = jnp.where(mine, target * share + slot_idx - my_y * share, -1)
    pick = (jnp.arange(owner_num * share, dtype=jnp.int32)[:, None] == place[None, :]).astype(BF16)
    tags = jnp.pad((action_ids + 1).astype(BF16), ((0, 0), (0, 128 - STEPS)))
    outgoing = jnp.dot(pick, jnp.concatenate([states, tags], 1), preferred_element_type=F32)
    outgoing = outgoing.astype(BF16).reshape(owner_num, share, width + 128)
    heads = lax.all_gather(head, "y", axis=0)

    g = grad_parts[0].reshape(NZ, NX, NC, rows, cols)
    parts = []
    for h in range(2):
        sl = slice(h * half, (h + 1) * half)
        gradient = reduce_part(g[..., sl])
        m_new = beta_one * moment_one[:, sl] + (1.0 - beta_one) * gradient
        v_new = beta_two * moment_two[:, sl] + (1.0 - beta_two) * gradient * gradient
        w_new = master[:, sl] - rate_lr * (m_new / corr_one) / (
            jnp.sqrt(v_new / corr_two) + adam_eps
        )
        parts.append((m_new, v_new, w_new, spread(w_new.astype(BF16), "z", NZ)))
    m_new, v_new, w_new = (jnp.concatenate([parts[0][i], parts[1][i]], 1) for i in range(3))
    wa, wb = parts[0][3], parts[1][3]
    wa, wb, outgoing = lax.optimization_barrier((wa, wb, outgoing))
    arrived = exchange(outgoing, DP)
    wa = spread(spread(wa, "x", NX), "y", NY)
    wb = spread(spread(wb, "y", NY), "x", NX)
    both = jnp.stack([wa, jnp.transpose(wb, (1, 0, 2, 3, 4))])
    other = swap(both)
    me = lax.axis_index("c")
    weights = jnp.where(me == 0, jnp.stack([both, other]), jnp.stack([other, both]))
    weights = jnp.transpose(weights, (4, 3, 0, 5, 2, 1, 6)).reshape(width, NY * cols)

    own = env_slots // NY
    arrived = arrived.reshape(owner_num * share, width + 128)
    slot_ids = arrived[:, width : width + STEPS].astype(jnp.int32) - 1
    env_ids = lax.dynamic_slice_in_dim(action_ids, my_y * own, own, 0)
    ids = jnp.concatenate([slot_ids, env_ids], 0)
    state = jnp.concatenate(
        [arrived[:, :width], lax.dynamic_slice_in_dim(states, my_y * own, own, 0)], 0
    )
    action_iota = jnp.arange(actions_num, dtype=jnp.int32)
    for step_idx in range(STEPS):
        onehot = (ids[:, step_idx][:, None] == action_iota[None, :]).astype(BF16)
        embedded = jnp.dot(onehot, act_table, preferred_element_type=F32)
        hidden = (state.astype(F32) + embedded).astype(BF16)
        mixed_f = jnp.dot(hidden, weights, preferred_element_type=F32).astype(BF16).astype(F32)
        inverse = lax.rsqrt(jnp.mean(mixed_f * mixed_f, axis=1) + norm_eps)
        state = (state.astype(F32) + norm_gain[None, :] * mixed_f * inverse[:, None]).astype(BF16)
    slots = owner_num * share
    kept = jnp.where(slot_ids[:, :1] >= 0, state[:slots], jnp.zeros((), BF16))
    landed = exchange(jnp.transpose(kept.reshape(slots, NY, cols), (1, 0, 2)), "y")
    row = jnp.arange(owner_num * capacity, dtype=jnp.int32)
    at = (row % capacity) // share * slots + row // capacity * share + row % share
    order = (at[:, None] == row[None, :]).astype(BF16)
    received = jnp.dot(order, landed.reshape(owner_num * capacity, cols), preferred_element_type=F32)

    scores = jnp.einsum("rd,jda->jra", state[slots:], heads, preferred_element_type=F32)
    scores = exchange(scores, "y").reshape(env_slots, head.shape[1])
    logits = scores * active[:, None].astype(F32)
    return (m_new, v_new, w_new, logits, received.astype(BF16))


def solution(mesh):
    grid = Mesh(mesh.devices.reshape(NZ, NX, NC, NY), DP + ("y",))
    in_specs = (
        P(DP, None, "y"),
        P(DP, "y"),
        P(DP, "y"),
        P(DP, "y"),
        P(DP, None),
        P(DP, None),
        P(DP),
        P(DP, None),
        P(),
        P(),
        P(None, "y"),
    )
    out_specs = (P(DP, "y"),) * 5
    return jax.shard_map(body, mesh=grid, in_specs=in_specs, out_specs=out_specs, check_vma=False)
```

time: 461 us -> 324 us (0.70)
  waiting for transfers between devices: 386 us -> 89.9 us
  starting transfers between devices: 11.3 us -> 55 us
  blocking collectives: 0 us -> 41.5 us
  local copies, waits for them, and re-layouts: 7.83 us -> 45.4 us
  matrix products: 20.7 us -> 40.3 us
  other arithmetic: 19.7 us -> 32.4 us
    all_gather x5 -> x1, waiting for transfers between devices: 212 us -> 24.7 us  [body(): heads = lax.all_gather(head, 'y', axis=0)]
    reduce_scatter x1 -> x0, waiting for transfers between devices: 147 us -> none  [body(): lax.psum_scatter(grad_parts[0], 'dp', scatter_dimension=0, tiled=True)]
    all_to_all x0 -> x3, blocking collectives: none -> 41.5 us  [exchange(): return lax.all_to_all(v, axis, 0, 0, tiled=True)]
    all_to_all x1 -> x10, waiting for transfers between devices: 26.5 us -> 63.5 us  [exchange(): return lax.all_to_all(v, axis, 0, 0, tiled=True)]
    all_to_all x1 -> x10, starting transfers between devices: 10.8 us -> 39.5 us  [exchange(): return lax.all_to_all(v, axis, 0, 0, tiled=True)]
    dot_general x5 -> x6, matrix products: 20.7 us -> 39.3 us  [the longest x4 35.3 us: body(): jnp.dot(hidden, weights, preferred_element_type=F32).astype(BF16)]
    ppermute x0 -> x3, starting transfers between devices: none -> 15.5 us  [swap(): return lax.ppermute(v, 'c', [(0, 1), (1, 0)])]
    reshape x2 -> x4, local copies, waits for them, and re-layouts: 4.21 us -> 18.2 us  [the longest x1 14.5 us: body(): jnp.transpose(weights, (4, 3, 0, 5, 2, 1, 6)).reshape(width, NY * cols)]
  transfers between devices with their start and end apart: 7 -> 14, of which waited for: 7 -> 12; matrix products, arithmetic and copies ran while one was open for 1% -> 8% of each run, Pallas kernels for 0% -> 0%
where the time goes in v1:
time: 324 us; the launch traced here: 320 us
  waiting for transfers between devices  89.9 us (28%)
  starting transfers between devices  55 us (17%)
  local copies, waits for them, and re-layouts  45.4 us (14%)
  blocking collectives  41.5 us (13%)
  matrix products  40.3 us (12%)
  other arithmetic  32.4 us (10%)
  between operations  15 us (5%)
    all_to_all x10, waiting for transfers between devices, exchange(): return lax.all_to_all(v, axis, 0, 0, tiled=True)  63.5 us
    all_to_all x3, blocking collectives, exchange(): return lax.all_to_all(v, axis, 0, 0, tiled=True)  41.5 us
    all_to_all x10, starting transfers between devices, exchange(): return lax.all_to_all(v, axis, 0, 0, tiled=True)  39.5 us
    dot_general x4, matrix products, body(): jnp.dot(hidden, weights, preferred_element_type=F32).astype(BF16)  35.3 us
    all_gather x1, waiting for transfers between devices, body(): heads = lax.all_gather(head, 'y', axis=0)  24.7 us
    ppermute x3, starting transfers between devices, swap(): return lax.ppermute(v, 'c', [(0, 1), (1, 0)])  15.5 us
    reshape x1, local copies, waits for them, and re-layouts, body(): jnp.transpose(weights, (4, 3, 0, 5, 2, 1, 6)).reshape(width, NY * cols)  14.5 us
    transpose x1, other arithmetic, body(): jnp.transpose(weights, (4, 3, 0, 5, 2, 1, 6)).reshape(width, NY * cols)  7.87 us
  transfers between devices with their start and end apart: 14, of which 12 were waited for; matrix products, arithmetic and copies ran while one was open for 8% of the time, Pallas kernels for 0%

profile of v1, /device:TPU:1, one launch (start us, length us, event | category | flops | bytes accessed | tf_op | source)
XLA Modules:
  0.0 319.7 jit_solution(17120212388826488211)
XLA Ops:
  7.2 4.1 %fusion.95 = (f32[8,4,2,32,256]{4,3,2,1,0:T(8,128)S(1)}, f32[8,4,2,32,256]{4,3,2,1,0:T(8,128)}) fusion(f32[8,4,2,32,512]{4,3,2,1,0:T(8,128)} %bitcast.92), kind=kLoop, calls=%fused_computation.170 | loop fusion | bytes 8388608 | tf_op jit(solution)/shard_map/slice | solution.py:85
  20.9 4.3 %all-to-all-start.2 = ((bf16[4,8,32,256]{3,2,1,0:T(8,128)(2,1)}), bf16[4,8,32,256]{3,2,1,0:T(8,128)(2,1)}, u32[]{:S(2)}, u32[]{:S(2)}) async-start(bf16[4,8,32,256]{3,2,1,0:T(8,128)(2,1)} %copy.66), calls=%async_computation.2 | async-start | bytes 1048576 | tf_op jit(solution)/shard_map/all_to_all | solution.py:22
  27.3 7.2 %all-to-all-done.2 = bf16[4,8,32,256]{3,2,1,0:T(8,128)(2,1)} async-done(((bf16[4,8,32,256]{3,2,1,0:T(8,128)(2,1)}), bf16[4,8,32,256]{3,2,1,0:T(8,128)(2,1)}, u32[]{:S(2)}, u32[]{:S(2)}) %all-to-all-start.2) | async-done | bytes 524320 | tf_op jit(solution)/shard_map/all_to_all | solution.py:22
  34.5 3.5 %all-to-all-start = ((bf16[4,8,32,256]{3,2,1,0:T(8,128)(2,1)}), bf16[4,8,32,256]{3,2,1,0:T(8,128)(2,1)S(1)}, u32[]{:S(2)}, u32[]{:S(2)}) async-start(bf16[4,8,32,256]{3,2,1,0:T(8,128)(2,1)} %copy.65), calls=%async_computation | async-start | bytes 1048576 | tf_op jit(solution)/shard_map/all_to_all | solution.py:22
  41.7 4.3 %all-to-all-done = bf16[4,8,32,256]{3,2,1,0:T(8,128)(2,1)S(1)} async-done(((bf16[4,8,32,256]{3,2,1,0:T(8,128)(2,1)}), bf16[4,8,32,256]{3,2,1,0:T(8,128)(2,1)S(1)}, u32[]{:S(2)}, u32[]{:S(2)}) %all-to-all-start) | async-done | bytes 524320 | tf_op jit(solution)/shard_map/all_to_all | solution.py:22
  46.0 6.0 %all-to-all-start.3 = ((bf16[8,32,256]{2,1,0:T(8,128)(2,1)}), bf16[8,32,256]{2,1,0:T(8,128)(2,1)S(1)}, u32[]{:S(2)}, u32[]{:S(2)}) async-start(bf16[8,32,256]{2,1,0:T(8,128)(2,1)} %reduce_sum.89), calls=%async_computation.3 | async-start | bytes 262144 | tf_op jit(solution)/shard_map/all_to_all | solution.py:22
  53.0 6.9 %all-to-all-done.3 = bf16[8,32,256]{2,1,0:T(8,128)(2,1)S(1)} async-done(((bf16[8,32,256]{2,1,0:T(8,128)(2,1)}), bf16[8,32,256]{2,1,0:T(8,128)(2,1)S(1)}, u32[]{:S(2)}, u32[]{:S(2)}) %all-to-all-start.3) | async-done | bytes 131104 | tf_op jit(solution)/shard_map/all_to_all | solution.py:22
  59.9 3.4 %all-to-all-start.1 = ((bf16[8,32,256]{2,1,0:T(8,128)(2,1)}), bf16[8,32,256]{2,1,0:T(8,128)(2,1)S(1)}, u32[]{:S(2)}, u32[]{:S(2)}) async-start(bf16[8,32,256]{2,1,0:T(8,128)(2,1)} %reduce_sum.87), calls=%async_computation.1 | async-start | bytes 262144 | tf_op jit(solution)/shard_map/all_to_all | solution.py:22
  63.3 7.8 %all-to-all-done.1 = bf16[8,32,256]{2,1,0:T(8,128)(2,1)S(1)} async-done(((bf16[8,32,256]{2,1,0:T(8,128)(2,1)}), bf16[8,32,256]{2,1,0:T(8,128)(2,1)S(1)}, u32[]{:S(2)}, u32[]{:S(2)}) %all-to-all-start.1) | async-done | bytes 131104 | tf_op jit(solution)/shard_map/all_to_all | solution.py:22
  72.5 3.4 %all-to-all-start.4 = ((bf16[8,32,256]{2,1,0:T(8,128)(2,1)}), bf16[8,32,256]{2,1,0:T(8,128)(2,1)S(1)}, u32[]{:S(2)}, u32[]{:S(2)}) async-start(bf16[8,32,256]{2,1,0:T(8,128)(2,1)} %broadcast_in_dim.24), calls=%async_computation.4 | async-start | bytes 262144 | tf_op jit(solution)/shard_map/all_to_all | solution.py:22
  76.2 7.5 %all-to-all-done.4 = bf16[8,32,256]{2,1,0:T(8,128)(2,1)S(1)} async-done(((bf16[8,32,256]{2,1,0:T(8,128)(2,1)}), bf16[8,32,256]{2,1,0:T(8,128)(2,1)S(1)}, u32[]{:S(2)}, u32[]{:S(2)}) %all-to-all-start.4) | async-done | bytes 131104 | tf_op jit(solution)/shard_map/all_to_all | solution.py:22
  91.2 4.3 %all-to-all-done.5 = bf16[8,32,256]{2,1,0:T(8,128)(2,1)S(1)} async-done(((bf16[8,32,256]{2,1,0:T(8,128)(2,1)}), bf16[8,32,256]{2,1,0:T(8,128)(2,1)S(1)}, u32[]{:S(2)}, u32[]{:S(2)}) %all-to-all-start.5) | async-done | bytes 131104 | tf_op jit(solution)/shard_map/all_to_all | solution.py:22
  95.6 10.9 %all_to_all.65 = bf16[4,8,32,256]{3,2,1,0:T(8,128)(2,1)S(1)} all-to-all(bf16[4,8,32,256]{3,2,1,0:T(8,128)(2,1)S(1)} %broadcast_in_dim.28), channel_id=1, replica_groups=mesh['z'=8,'x'=4,'c'=2,'y'=4] {'y'}, dimensions={0} | all-to-all | bytes 1048576 | tf_op jit(solution)/shard_map/all_to_all | solution.py:22
  106.6 9.3 %all_to_all.66 = bf16[4,8,32,256]{3,2,1,0:T(8,128)(2,1)S(1)} all-to-all(bf16[4,8,32,256]{3,2,1,0:T(8,128)(2,1)S(1)} %broadcast_in_dim.26), channel_id=1, replica_groups=mesh['z'=8,'x'=4,'c'=2,'y'=4] {'x'}, dimensions={0} | all-to-all | bytes 1048576 | tf_op jit(solution)/shard_map/all_to_all | solution.py:22
  116.2 21.2 %all_to_all.67 = bf16[4,4,8,32,256]{4,3,2,1,0:T(8,128)(2,1)S(1)} all-to-all(bf16[4,4,8,32,256]{4,3,2,1,0:T(8,128)(2,1)S(1)} %broadcast_in_dim.29), channel_id=1, replica_groups=mesh['z'=8,'x'=4,'c'=2,'y'=4] {'x'}, dimensions={0} | all-to-all | bytes 4194304 | tf_op jit(solution)/shard_map/all_to_all | solution.py:22
  139.1 4.5 %all-to-all-start.8 = ((bf16[4,4,8,32,256]{4,3,2,1,0:T(8,128)(2,1)}), bf16[4,4,8,32,256]{4,3,2,1,0:T(8,128)(2,1)}, u32[]{:S(2)}, u32[]{:S(2)}) async-start(bf16[4,4,8,32,256]{4,3,2,1,0:T(8,128)(2,1)} %broadcast_in_dim.27), calls=%async_computation.8 | async-start | bytes 4194304 | tf_op jit(solution)/shard_map/all_to_all | solution.py:22
  145.1 13.9 %all-to-all-done.8 = bf16[4,4,8,32,256]{4,3,2,1,0:T(8,128)(2,1)} async-done(((bf16[4,4,8,32,256]{4,3,2,1,0:T(8,128)(2,1)}), bf16[4,4,8,32,256]{4,3,2,1,0:T(8,128)(2,1)}, u32[]{:S(2)}, u32[]{:S(2)}) %all-to-all-start.8) | async-done | bytes 2097184 | tf_op jit(solution)/shard_map/all_to_all | solution.py:22
  159.0 5.0 %fusion.90 = (bf16[1,2,4,4,8,32,256]{6,5,4,3,2,1,0:T(8,128)(2,1)}, bf16[2,4,4,8,32,256]{5,4,3,2,1,0:T(8,128)(2,1)}) fusion(bf16[1,4,4,8,32,256]{5,4,3,2,1,0:T(8,128)(2,1)} %bitcast.91, bf16[1,4,4,8,32,256]{5,4,3,2,1,0:T(8,128)(2,1)} %bitcast.11), kind=kLoop, calls=%fused_computation.167 | loop fusion | flops 2097152 | bytes 12582912 | tf_op jit(solution)/shard_map/stack | solution.py:101
  164.0 12.3 %collective-permute-start.2 = (bf16[2,4,4,8,32,256]{5,4,3,2,1,0:T(8,128)(2,1)}, bf16[2,4,4,8,32,256]{5,4,3,2,1,0:T(8,128)(2,1)}, u32[]{:S(2)}, u32[]{:S(2)}) collective-permute-start(bf16[2,4,4,8,32,256]{5,4,3,2,1,0:T(8,128)(2,1)} %get-tuple-element.24), channel_id=1, source_target_pairs={{0,4},{4,0},{1,5},{5,1},{2,6},{6,2},{3,7},{7,3},{8,12},{12,8},{9,1... | collective-permute-start | bytes 12582920 | tf_op jit(solution)/shard_map/ppermute | solution.py:30
  176.3 4.2 %all-to-all-start.6 = ((bf16[64,3,2176]{2,1,0:T(4,128)(2,1)}), bf16[64,3,2176]{2,1,0:T(4,128)(2,1)S(1)}, u32[]{:S(2)}, u32[]{:S(2)}) async-start(bf16[64,3,2176]{2,1,0:T(4,128)(2,1)} %reshape.148), calls=%async_computation.6 | async-start | bytes 2228224 | tf_op jit(solution)/shard_map/all_to_all | solution.py:22
  183.1 24.7 %all-gather.3.cloned.1.call-done = bf16[8192,64]{0,1:T(8,128)(2,1)} async-done(((bf16[2048,64]{0,1:T(8,128)(2,1)}), bf16[8192,64]{0,1:T(8,128)(2,1)}) %all-gather.3.cloned.1.call-update) | async-done | bytes 1048592 | tf_op jit(solution)/shard_map/all_gather | solution.py:79
  214.7 7.9 %fusion = bf16[8,4,2,32,4,2,256]{6,3,0,1,4,5,2:T(8,128)(2,1)S(1)} fusion(bf16[1,2,4,4,8,32,256]{6,5,4,3,2,1,0:T(8,128)(2,1)} %bitcast.15, bf16[1,2,4,4,8,32,256]{6,5,4,3,2,1,0:T(8,128)(2,1)} %get-tuple-element.23, pred[]{:T(512)S(6)} %eq.144), kind=kLoop, calls=%fused_computation.1 | loop fusion | flops 12582912 | bytes 16777216 | tf_op jit(solution)/shard_map/transpose | solution.py:102
  222.6 7.8 %copy.71 = bf16[8,4,2,32,4,2,256]{6,5,4,3,2,1,0:T(2,128)(2,1)} copy(bf16[8,4,2,32,4,2,256]{6,3,0,1,4,5,2:T(8,128)(2,1)S(1)} %fusion) | data formatting | bytes 16777216 | tf_op jit(solution)/shard_map/transpose | solution.py:102
  230.4 14.5 %reshape.150 = bf16[2048,2048]{1,0:T(8,128)(2,1)} reshape(bf16[8,4,2,32,4,2,256]{6,5,4,3,2,1,0:T(2,128)(2,1)} %copy.71) | data formatting | bytes 16777216 | tf_op jit(solution)/shard_map/reshape | solution.py:102
  244.9 8.4 %fusion.8 = (f32[320]{0:T(512)}, bf16[320,2048]{1,0:T(8,128)(2,1)}) fusion(bf16[2048,2048]{1,0:T(8,128)(2,1)} %reshape.150, bf16[256,2048]{1,0:T(8,128)(2,1)S(1)} %copy-done, bf16[128,2048]{1,0:T(8,128)(2,1)S(1)} %copy-done.3, bf16[192,2048]{1,0:T(8,128)(2,1)S(1)} %slice.79, s32[320]{0:T(512)S(1)} %get-tuple-element.12), kind=kOutput, calls=%fused_computation.32 | convolution fusion | flops 3026534144 | bytes 12061184 | tf_op jit(solution)/shard_map/dot_general | solution.py:117
  254.0 9.0 %fusion.11 = (f32[320]{0:T(512)}, bf16[320,2048]{1,0:T(8,128)(2,1)}) fusion(bf16[2048,2048]{1,0:T(8,128)(2,1)} %reshape.150, bf16[256,2048]{1,0:T(8,128)(2,1)S(1)} %copy-done, s32[320]{0:T(512)} %get-tuple-element.13, f32[320]{0:T(512)S(1)} %add_rsqrt_fusion.3, bf16[320,2048]{1,0:T(8,128)(2,1)} %get-tuple-element.32, f32[2048]{0:T(1024)S(1)} %copy-done.9, ...), kind=kOutput, calls=%fused_computation.35 | convolution fusion | flops 3030466304 | bytes 13381376 | tf_op jit(solution)/shard_map/dot_general | solution.py:117
  266.7 8.9 %fusion.14 = (f32[320]{0:T(512)}, bf16[320,2048]{1,0:T(8,128)(2,1)}) fusion(bf16[2048,2048]{1,0:T(8,128)(2,1)} %reshape.150, bf16[256,2048]{1,0:T(8,128)(2,1)S(1)} %copy-done, bf16[320,2048]{1,0:T(8,128)(2,1)S(1)} %fusion.9, s32[320]{0:T(512)} %get-tuple-element.11), kind=kOutput, calls=%fused_computation.38 | convolution fusion | flops 3024568064 | bytes 12061184 | tf_op jit(solution)/shard_map/dot_general | solution.py:117
  276.2 9.0 %fusion.17 = (f32[320]{0:T(512)}, bf16[320,2048]{1,0:T(8,128)(2,1)}) fusion(bf16[2048,2048]{1,0:T(8,128)(2,1)} %reshape.150, bf16[256,2048]{1,0:T(8,128)(2,1)S(1)} %copy-done, s32[320]{0:T(512)S(1)} %get-tuple-element.14, f32[320]{0:T(512)S(1)} %add_rsqrt_fusion.1, bf16[320,2048]{1,0:T(8,128)(2,1)} %get-tuple-element.36, f32[2048]{0:T(1024)S(1)} %copy-done.9, ...), kind=kOutput, calls=%fused_computation.41 | convolution fusion | flops 3028500224 | bytes 13381376 | tf_op jit(solution)/shard_map/dot_general | solution.py:117
  290.0 3.5 %all-to-all-start.11 = ((f32[4,128,64]{1,2,0:T(8,128)}), f32[4,128,64]{1,2,0:T(8,128)S(1)}, u32[]{:S(2)}, u32[]{:S(2)}) async-start(f32[4,128,64]{1,2,0:T(8,128)} %bitcast.20), calls=%async_computation.11 | async-start | bytes 262144 | tf_op jit(solution)/shard_map/all_to_all | solution.py:22
  294.6 3.7 %all-to-all-done.11 = f32[4,128,64]{1,2,0:T(8,128)S(1)} async-done(((f32[4,128,64]{1,2,0:T(8,128)}), f32[4,128,64]{1,2,0:T(8,128)S(1)}, u32[]{:S(2)}, u32[]{:S(2)}) %all-to-all-start.11) | async-done | bytes 131104 | tf_op jit(solution)/shard_map/all_to_all | solution.py:22
  298.3 3.5 %all-to-all-start.12 = ((bf16[4,192,512]{2,1,0:T(8,128)(2,1)}), bf16[4,192,512]{2,1,0:T(8,128)(2,1)S(1)}, u32[]{:S(2)}, u32[]{:S(2)}) async-start(bf16[4,192,512]{2,1,0:T(8,128)(2,1)} %bitcast.86), calls=%async_computation.12 | async-start | bytes 1572864 | tf_op jit(solution)/shard_map/all_to_all | solution.py:22
  303.8 7.4 %all-to-all-done.12 = bf16[4,192,512]{2,1,0:T(8,128)(2,1)S(1)} async-done(((bf16[4,192,512]{2,1,0:T(8,128)(2,1)}), bf16[4,192,512]{2,1,0:T(8,128)(2,1)S(1)}, u32[]{:S(2)}, u32[]{:S(2)}) %all-to-all-start.12) | async-done | bytes 786464 | tf_op jit(solution)/shard_map/all_to_all | solution.py:22
  (91 shorter events, 52.5 us)
Async XLA Ops:
  7.2 237.7 %copy-start = (bf16[256,2048]{1,0:T(8,128)(2,1)S(1)}, bf16[256,2048]{1,0:T(8,128)(2,1)}, u32[]{:S(2)}) copy-start(bf16[256,2048]{1,0:T(8,128)(2,1)} %param.19) | copy-start | bytes 3145732
  13.4 5.1 %collective-permute-start.1 = (bf16[8,4,32,256]{3,2,1,0:T(8,128)(2,1)}, bf16[8,4,32,256]{3,2,1,0:T(8,128)(2,1)}, u32[]{:S(2)}, u32[]{:S(2)}) collective-permute-start(bf16[8,4,32,256]{3,2,1,0:T(8,128)(2,1)} %fusion.30), channel_id=1, source_target_pairs={{0,4},{4,0},{1,5},{5,1},{2,6},{6,2},{3,7},{7,3},{8,12},{12,8},{9,1... | collective-permute-start | bytes 1572872 | tf_op jit(solution)/shard_map/ppermute | solution.py:30
  17.5 7.7 %collective-permute-start = (bf16[8,4,32,256]{3,2,1,0:T(8,128)(2,1)}, bf16[8,4,32,256]{3,2,1,0:T(8,128)(2,1)}, u32[]{:S(2)}, u32[]{:S(2)}) collective-permute-start(bf16[8,4,32,256]{3,2,1,0:T(8,128)(2,1)} %fusion.29), channel_id=1, source_target_pairs={{0,4},{4,0},{1,5},{5,1},{2,6},{6,2},{3,7},{7,3},{8,12},{12,8},{9,1... | collective-permute-start | bytes 1572872 | tf_op jit(solution)/shard_map/ppermute | solution.py:30
  20.9 17.7 %copy-start.10 = (s32[512,1]{0,1:T(1,128)S(1)}, s32[512,1]{0,1:T(1,128)}, u32[]{:S(2)}) copy-start(s32[512,1]{0,1:T(1,128)} %param.18) | copy-start | bytes 6148
  20.9 13.6 %all-to-all-start.2 = ((bf16[4,8,32,256]{3,2,1,0:T(8,128)(2,1)}), bf16[4,8,32,256]{3,2,1,0:T(8,128)(2,1)}, u32[]{:S(2)}, u32[]{:S(2)}) async-start(bf16[4,8,32,256]{3,2,1,0:T(8,128)(2,1)} %copy.66), calls=%async_computation.2 | async-start | bytes 1048576 | tf_op jit(solution)/shard_map/all_to_all | solution.py:22
  25.2 27.0 %copy-start.11 = (s32[512,4]{0,1:T(4,128)S(1)}, s32[512,4]{0,1:T(4,128)}, u32[]{:S(2)}) copy-start(s32[512,4]{0,1:T(4,128)} %param.16) | copy-start | bytes 24580
  26.5 44.6 %copy-start.6 = (f32[32,512]{1,0:T(8,128)S(1)}, f32[32,512]{1,0:T(8,128)}, u32[]{:S(2)}) copy-start(f32[32,512]{1,0:T(8,128)} %param.12) | copy-start | bytes 196612
  26.5 44.6 %copy-start.7 = (f32[32,512]{1,0:T(8,128)S(1)}, f32[32,512]{1,0:T(8,128)}, u32[]{:S(2)}) copy-start(f32[32,512]{1,0:T(8,128)} %param.14) | copy-start | bytes 196612
  26.5 44.6 %copy-start.8 = (f32[32,512]{1,0:T(8,128)S(1)}, f32[32,512]{1,0:T(8,128)}, u32[]{:S(2)}) copy-start(f32[32,512]{1,0:T(8,128)} %param.13) | copy-start | bytes 196612
  34.5 11.5 %all-to-all-start = ((bf16[4,8,32,256]{3,2,1,0:T(8,128)(2,1)}), bf16[4,8,32,256]{3,2,1,0:T(8,128)(2,1)S(1)}, u32[]{:S(2)}, u32[]{:S(2)}) async-start(bf16[4,8,32,256]{3,2,1,0:T(8,128)(2,1)} %copy.65), calls=%async_computation | async-start | bytes 1048576 | tf_op jit(solution)/shard_map/all_to_all | solution.py:22
  46.0 13.9 %all-to-all-start.3 = ((bf16[8,32,256]{2,1,0:T(8,128)(2,1)}), bf16[8,32,256]{2,1,0:T(8,128)(2,1)S(1)}, u32[]{:S(2)}, u32[]{:S(2)}) async-start(bf16[8,32,256]{2,1,0:T(8,128)(2,1)} %reduce_sum.89), calls=%async_computation.3 | async-start | bytes 262144 | tf_op jit(solution)/shard_map/all_to_all | solution.py:22
  59.9 11.2 %all-to-all-start.1 = ((bf16[8,32,256]{2,1,0:T(8,128)(2,1)}), bf16[8,32,256]{2,1,0:T(8,128)(2,1)S(1)}, u32[]{:S(2)}, u32[]{:S(2)}) async-start(bf16[8,32,256]{2,1,0:T(8,128)(2,1)} %reduce_sum.87), calls=%async_computation.1 | async-start | bytes 262144 | tf_op jit(solution)/shard_map/all_to_all | solution.py:22
  72.5 11.2 %all-to-all-start.4 = ((bf16[8,32,256]{2,1,0:T(8,128)(2,1)}), bf16[8,32,256]{2,1,0:T(8,128)(2,1)S(1)}, u32[]{:S(2)}, u32[]{:S(2)}) async-start(bf16[8,32,256]{2,1,0:T(8,128)(2,1)} %broadcast_in_dim.24), calls=%async_computation.4 | async-start | bytes 262144 | tf_op jit(solution)/shard_map/all_to_all | solution.py:22
  84.3 11.2 %all-to-all-start.5 = ((bf16[8,32,256]{2,1,0:T(8,128)(2,1)}), bf16[8,32,256]{2,1,0:T(8,128)(2,1)S(1)}, u32[]{:S(2)}, u32[]{:S(2)}) async-start(bf16[8,32,256]{2,1,0:T(8,128)(2,1)} %broadcast_in_dim.25), calls=%async_computation.5 | async-start | bytes 262144 | tf_op jit(solution)/shard_map/all_to_all | solution.py:22
  139.1 19.9 %all-to-all-start.8 = ((bf16[4,4,8,32,256]{4,3,2,1,0:T(8,128)(2,1)}), bf16[4,4,8,32,256]{4,3,2,1,0:T(8,128)(2,1)}, u32[]{:S(2)}, u32[]{:S(2)}) async-start(bf16[4,4,8,32,256]{4,3,2,1,0:T(8,128)(2,1)} %broadcast_in_dim.27), calls=%async_computation.8 | async-start | bytes 4194304 | tf_op jit(solution)/shard_map/all_to_all | solution.py:22
  164.0 50.7 %collective-permute-start.2 = (bf16[2,4,4,8,32,256]{5,4,3,2,1,0:T(8,128)(2,1)}, bf16[2,4,4,8,32,256]{5,4,3,2,1,0:T(8,128)(2,1)}, u32[]{:S(2)}, u32[]{:S(2)}) collective-permute-start(bf16[2,4,4,8,32,256]{5,4,3,2,1,0:T(8,128)(2,1)} %get-tuple-element.24), channel_id=1, source_target_pairs={{0,4},{4,0},{1,5},{5,1},{2,6},{6,2},{3,7},{7,3},{8,12},{12,8},{9,1... | collective-permute-start | bytes 12582920 | tf_op jit(solution)/shard_map/ppermute | solution.py:30
  176.3 33.5 %all-to-all-start.6 = ((bf16[64,3,2176]{2,1,0:T(4,128)(2,1)}), bf16[64,3,2176]{2,1,0:T(4,128)(2,1)S(1)}, u32[]{:S(2)}, u32[]{:S(2)}) async-start(bf16[64,3,2176]{2,1,0:T(4,128)(2,1)} %reshape.148), calls=%async_computation.6 | async-start | bytes 2228224 | tf_op jit(solution)/shard_map/all_to_all | solution.py:22
  180.5 27.4 %all-gather.3.cloned.1.call-start = ((), (), s32[]{:S(2)}) async-start(), calls=%async_computation.13 | async-start | bytes 1310720 | tf_op jit(solution)/shard_map/all_gather | solution.py:79
  212.5 41.5 %copy-start.2 = (bf16[192,2048]{1,0:T(8,128)(2,1)}, bf16[192,2048]{1,0:T(8,128)(2,1)S(1)}, u32[]{:S(2)}) copy-start(bf16[192,2048]{1,0:T(8,128)(2,1)S(1)} %slice.79) | copy-start | bytes 2359300
  230.4 14.5 %copy-start.3 = (bf16[128,2048]{1,0:T(8,128)(2,1)S(1)}, bf16[128,2048]{1,0:T(8,128)(2,1)}, u32[]{:S(2)}) copy-start(bf16[128,2048]{1,0:T(8,128)(2,1)} %constant_dynamic-slice_fusion.1) | copy-start | bytes 1572868
  244.9 9.1 %copy-start.9 = (f32[2048]{0:T(1024)S(1)}, f32[2048]{0:T(1024)}, u32[]{:S(2)}) copy-start(f32[2048]{0:T(1024)} %param.20) | copy-start | bytes 24580
  266.7 9.6 %copy-start.1 = (bf16[320,2048]{1,0:T(8,128)(2,1)}, bf16[320,2048]{1,0:T(8,128)(2,1)S(1)}, u32[]{:S(2)}) copy-start(bf16[320,2048]{1,0:T(8,128)(2,1)S(1)} %fusion.9) | copy-start | bytes 3932164
  285.9 7.5 %copy-start.12 = (pred[192]{0:T(512)(128)(4,1)S(1)}, pred[192]{0:T(512)(128)(4,1)}, u32[]{:S(2)}) copy-start(pred[192]{0:T(512)(128)(4,1)} %compare_reduce_fusion) | copy-start | bytes 580
  290.0 12.4 %copy-start.4 = (f32[32,256]{1,0:T(8,128)S(1)}, f32[32,256]{1,0:T(8,128)}, u32[]{:S(2)}) copy-start(f32[32,256]{1,0:T(8,128)} %get-tuple-element.29) | copy-start | bytes 98308
  290.0 12.4 %copy-start.5 = (f32[32,256]{1,0:T(8,128)S(1)}, f32[32,256]{1,0:T(8,128)}, u32[]{:S(2)}) copy-start(f32[32,256]{1,0:T(8,128)} %get-tuple-element.30) | copy-start | bytes 98308
  290.0 8.3 %all-to-all-start.11 = ((f32[4,128,64]{1,2,0:T(8,128)}), f32[4,128,64]{1,2,0:T(8,128)S(1)}, u32[]{:S(2)}, u32[]{:S(2)}) async-start(f32[4,128,64]{1,2,0:T(8,128)} %bitcast.20), calls=%async_computation.11 | async-start | bytes 262144 | tf_op jit(solution)/shard_map/all_to_all | solution.py:22
  298.3 12.9 %all-to-all-start.12 = ((bf16[4,192,512]{2,1,0:T(8,128)(2,1)}), bf16[4,192,512]{2,1,0:T(8,128)(2,1)S(1)}, u32[]{:S(2)}, u32[]{:S(2)}) async-start(bf16[4,192,512]{2,1,0:T(8,128)(2,1)} %bitcast.86), calls=%async_computation.12 | async-start | bytes 1572864 | tf_op jit(solution)/shard_map/all_to_all | solution.py:22
Sparse Core Ops, SparseCore 0:
  183.1 24.6 all-gather.2

commit v2 on v1

v2 whole, which is shorter than its diff:
```python
import functools

import jax
import jax.numpy as jnp
from jax import lax
from jax.experimental import pallas as pl
from jax.experimental.pallas import tpu as pltpu
from jax.sharding import Mesh, PartitionSpec as P

STEPS = 4
NZ, NX, NC, NY = 8, 4, 2, 4
DP = ("z", "x", "c")
TAGS = 128

beta_one = 0.9
beta_two = 0.999
corr_one = 1.0 - 0.9**10
corr_two = 1.0 - 0.999**10
rate_lr = 0.01
adam_eps = 1e-08
norm_eps = 1e-06
F32 = jnp.float32
BF16 = jnp.bfloat16


def exchange(v, axis):
    return lax.all_to_all(v, axis, 0, 0, tiled=True)


def shift(v, axis, k, n):
    if k == 0:
        return v
    return lax.ppermute(v, axis, [(i, (i + k) % n) for i in range(n)])


def swap(v):
    return shift(v, "c", 1, NC)


def give_kernel(where, g_ref, out_ref):
    out_ref[0] = g_ref[:, 0, 0].astype(BF16)


def keep_kernel(where, g_ref, got_ref, out_ref):
    out_ref[0] = (g_ref[:, 0, 0] + got_ref[0].astype(F32)).astype(BF16)


def rows_of_core(kernel, core, g, *rest):
    nz, nx, _, rows, cols = g.shape
    block = pl.BlockSpec((1, nz, rows, cols), lambda i, where: (i, 0, 0, 0))
    return pl.pallas_call(
        kernel,
        grid_spec=pltpu.PrefetchScalarGridSpec(
            num_scalar_prefetch=1,
            grid=(nx,),
            in_specs=[
                pl.BlockSpec((nz, 1, 1, rows, cols), lambda i, where: (0, i, where[0], 0, 0)),
                *[block for _ in rest],
            ],
            out_specs=block,
        ),
        out_shape=jax.ShapeDtypeStruct((nx, nz, rows, cols), BF16),
        compiler_params=pltpu.CompilerParams(vmem_limit_bytes=24 * 2**20),
    )(core, g, *rest)


def decode_kernel(with_logits, m, width, place, rows_ref, table_ref, gain_ref, *refs):
    n_pieces = 4 * NY
    if with_logits:
        head_ref, refs = refs[0], refs[1:]
    pieces, (out_ref, w_ref, hidden, mixed, state, sems) = refs[:n_pieces], refs[n_pieces:]
    my_x, my_c, my_y = place[0], place[1], place[2]
    blocks, wide = w_ref.shape[0], w_ref.shape[-1]
    copies = []
    for p in range(n_pieces):
        second, k, other = p // (2 * NY), p % (2 * NY) // 2, p % 2
        core = lax.rem(my_c + other, NC)
        for i in range(NX):
            x_off, y_off = (k, i) if second else (i, k)
            x = lax.rem(my_x - x_off + NX, NX)
            y = lax.rem(my_y - y_off + NY, NY)
            copy = pltpu.make_async_copy(
                pieces[p].at[i], w_ref.at[2 * y + second, :, x, core], sems.at[p * NX + i]
            )
            copy.start()
            copies.append(copy)

    actions = table_ref.shape[0]
    number = lax.broadcasted_iota(jnp.int32, (m, actions), 1) + 1

    def embed(step, n, old):
        tag = rows_ref[:, width + step : width + step + 1].astype(jnp.int32)
        onehot = jnp.where(tag == number, 1.0, 0.0).astype(BF16)
        at = pl.ds(n * wide, wide)
        embedded = jnp.dot(onehot, table_ref[:, at], preferred_element_type=F32)
        hidden[:, at] = (old.astype(F32) + embedded).astype(BF16)

    for n in range(blocks):
        embed(0, n, rows_ref[:, n * wide : (n + 1) * wide])
    for copy in copies:
        copy.wait()
    for step in range(STEPS):

        def multiply(i, total):
            for half in range(2):
                n = 2 * i + half
                w = w_ref[n].reshape(width, wide)
                got = jnp.dot(hidden[...], w, preferred_element_type=F32).astype(BF16)
                mixed[:, pl.ds(pl.multiple_of(n * wide, wide), wide)] = got
                got = got.astype(F32)
                total = total + jnp.sum(got * got, axis=1, keepdims=True)
            return total

        total = lax.fori_loop(0, blocks // 2, multiply, jnp.zeros((m, 1), F32))
        inverse = lax.rsqrt(total * (1.0 / width) + norm_eps)
        for n in range(blocks):
            at = slice(n * wide, (n + 1) * wide)
            old = rows_ref[:, at] if step == 0 else state[:, at]
            new = old.astype(F32) + gain_ref[:, at] * mixed[:, at].astype(F32) * inverse
            new = new.astype(BF16)
            if step < STEPS - 1:
                state[:, at] = new
                embed(step + 1, n, new)
            elif with_logits:
                state[:, at] = new
            else:
                k = lax.rem(n // 2 - my_y + NY, NY)
                out_ref[k, :, n % 2 * wide : (n % 2 + 1) * wide] = new
    if with_logits:
        scores = jnp.dot(state[...], head_ref[...], preferred_element_type=F32)
        row = my_y * m + lax.broadcasted_iota(jnp.int32, scores.shape, 0)
        out_ref[...] = scores * jnp.where(row < place[3], 1.0, 0.0)


def decode(place, rows, table, gain, pieces, head=None):
    m, width = rows.shape[0], table.shape[1]
    wide = width // NY // 2
    vmem = pl.BlockSpec(memory_space=pltpu.VMEM)
    if head is None:
        out = jax.ShapeDtypeStruct((NY, m, width // NY), BF16)
    else:
        out = jax.ShapeDtypeStruct((m, head.shape[1]), F32)
    extra = [] if head is None else [head]
    return pl.pallas_call(
        functools.partial(decode_kernel, head is not None, m, width),
        in_specs=[pl.BlockSpec(memory_space=pltpu.SMEM)]
        + [vmem] * (3 + len(extra))
        + [pl.BlockSpec(memory_space=pl.ANY)] * len(pieces),
        out_specs=vmem,
        out_shape=out,
        scratch_shapes=[
            pltpu.VMEM((2 * NY, NZ, NX, NC, width // (NZ * NX * NC), wide), BF16),
            pltpu.VMEM((m, width), BF16),
            pltpu.VMEM((m, width), BF16),
            pltpu.VMEM((m, width), BF16),
            pltpu.SemaphoreType.DMA((len(pieces) * NX,)),
        ],
        compiler_params=pltpu.CompilerParams(vmem_limit_bytes=32 * 2**20),
        cost_estimate=pl.CostEstimate(
            flops=2 * STEPS * m * width * width, bytes_accessed=2 * width * width, transcendentals=0
        ),
    )(place, rows, table, gain, *extra, *pieces)


def body(
    grad_parts,
    master,
    moment_one,
    moment_two,
    states,
    action_ids,
    env_counts,
    owners,
    act_table,
    norm_gain,
    head,
):
    width, cols = grad_parts.shape[1:]
    rows = width // (NZ * NX * NC)
    half = cols // 2
    env_slots = states.shape[0]
    owner_num = NZ * NX * NC
    capacity = max(2, 3 * env_slots // (2 * owner_num))
    share = capacity // NY
    slots = owner_num * share
    own = env_slots // NY
    my_x, my_c, my_y = lax.axis_index("x"), lax.axis_index("c"), lax.axis_index("y")
    place = jnp.stack([my_x, my_c, my_y, env_counts[0]]).astype(jnp.int32)

    g = grad_parts[0].reshape(NZ, NX, NC, rows, cols)
    got = swap(rows_of_core(give_kernel, (1 - my_c)[None].astype(jnp.int32), g))
    both = rows_of_core(keep_kernel, my_c[None].astype(jnp.int32), g, got)
    by_x = exchange(both, "x").astype(F32).sum(0).astype(BF16)
    gradient = exchange(by_x, "z").astype(F32).sum(0)

    heads = jnp.concatenate([shift(head, "y", (NY - k) % NY, NY) for k in range(NY)], 1)

    active = jnp.arange(env_slots, dtype=jnp.int32) < env_counts[0]
    target = owners[:, 0]
    marks = (
        (target[:, None] == jnp.arange(owner_num, dtype=jnp.int32)[None, :]) & active[:, None]
    ).astype(jnp.int32)
    ranked = jnp.cumsum(marks, axis=0) - marks
    slot_idx = jnp.sum(ranked * marks, axis=1)
    mine = active & (slot_idx // share == my_y)
    index = jnp.where(mine, target * share + slot_idx - my_y * share, -1)
    pick = (jnp.arange(slots, dtype=jnp.int32)[:, None] == index[None, :]).astype(BF16)
    tags = jnp.pad((action_ids + 1).astype(BF16), ((0, 0), (0, TAGS - STEPS)))
    tagged = jnp.concatenate([states, tags], 1)
    outgoing = jnp.dot(pick, tagged, preferred_element_type=F32)
    outgoing = outgoing.astype(BF16).reshape(owner_num, share, width + TAGS)
    actor_rows = lax.dynamic_slice_in_dim(tagged, my_y * own, own, 0)

    m_new = beta_one * moment_one + (1.0 - beta_one) * gradient
    v_new = beta_two * moment_two + (1.0 - beta_two) * gradient * gradient
    w_new = master - rate_lr * (m_new / corr_one) / (jnp.sqrt(v_new / corr_two) + adam_eps)

    w = exchange(jnp.broadcast_to(w_new.astype(BF16)[None], (NZ, rows, cols)), "z")
    w, outgoing, actor_rows, heads = lax.optimization_barrier((w, outgoing, actor_rows, heads))
    first, second = w[..., :half], w[..., half:]
    first = jnp.stack([shift(first, "x", k, NX) for k in range(NX)])
    second = jnp.stack([shift(second, "y", k, NY) for k in range(NY)])
    arrived = exchange(outgoing, DP)
    pieces = []
    for v, axis, n in ((first, "y", NY), (second, "x", NX)):
        for k in range(n):
            piece = shift(v, axis, k, n)
            pieces += [piece, swap(piece)]

    slot_rows = arrived.reshape(slots, width + TAGS)
    gain = norm_gain[None, :]
    final = decode(place, slot_rows, act_table, gain, pieces)
    final, actor_rows = lax.optimization_barrier((final, actor_rows))
    landed = [shift(final[k], "y", k, NY) for k in range(NY)]
    scores = decode(place, actor_rows, act_table, gain, pieces, heads)

    each = head.shape[1]
    scores = [shift(scores[:, k * each : (k + 1) * each], "y", k, NY) for k in range(NY)]
    logits = jnp.zeros((env_slots, each), F32)
    for k in range(NY):
        start = lax.rem(my_y - k + NY, NY) * own
        logits = lax.dynamic_update_slice_in_dim(logits, scores[k], start, 0)

    row = jnp.arange(owner_num * capacity, dtype=jnp.int32)
    part = lax.rem(my_y - row % capacity // share + NY, NY)
    at = part * slots + row // capacity * share + row % share
    order = (at[:, None] == row[None, :]).astype(BF16)
    received = jnp.dot(order, jnp.concatenate(landed, 0), preferred_element_type=F32)
    return (m_new, v_new, w_new, logits, received.astype(BF16))


def solution(mesh):
    grid = Mesh(mesh.devices.reshape(NZ, NX, NC, NY), DP + ("y",))
    in_specs = (
        P(DP, None, "y"),
        P(DP, "y"),
        P(DP, "y"),
        P(DP, "y"),
        P(DP, None),
        P(DP, None),
        P(DP),
        P(DP, None),
        P(),
        P(),
        P(None, "y"),
    )
    out_specs = (P(DP, "y"),) * 5
    return jax.shard_map(body, mesh=grid, in_specs=in_specs, out_specs=out_specs, check_vma=False)
```

time: 324 us -> 216 us (0.67)
  blocking collectives: 41.5 us -> 0 us
  matrix products: 40.3 us -> 3.25 us
  Pallas kernels: 0 us -> 33.6 us
  other arithmetic: 32.4 us -> 7.32 us
  local copies, waits for them, and re-layouts: 45.4 us -> 25.6 us
  between operations: 15 us -> 1.8 us
  waiting for transfers between devices: 89.9 us -> 83.9 us
  starting transfers between devices: 55 us -> 59.3 us
    ppermute x3 -> x30, waiting for transfers between devices: 1.01 us -> 61.2 us  [shift(): return lax.ppermute(v, axis, [(i, (i + k) % n) for i in range(n)])]
    all_to_all x3 -> x0, blocking collectives: 41.5 us -> none  [exchange(): return lax.all_to_all(v, axis, 0, 0, tiled=True)]
    all_to_all x10 -> x4, waiting for transfers between devices: 63.5 us -> 22.7 us  [exchange(): return lax.all_to_all(v, axis, 0, 0, tiled=True)]
    dot_general x6 -> x2, matrix products: 39.3 us -> 3.25 us  [the longest x1 1.69 us: body(): jnp.dot(order, jnp.concatenate(landed, 0), preferred_element_type=F32)]
    pallas_call x0 -> x4, Pallas kernels: none -> 33.6 us  [the longest x2 31.5 us: decode(): pl.pallas_call(functools.partial(decode_kernel, head is not None, m, widt...]
    all_gather x1 -> x0, waiting for transfers between devices: 24.7 us -> none  [body(): heads = lax.all_gather(head, 'y', axis=0)]
    unnamed x28 -> x63, local copies, waits for them, and re-layouts: 0.33 us -> 18.1 us
    ppermute x3 -> x30, starting transfers between devices: 15.5 us -> 32.5 us  [shift(): return lax.ppermute(v, axis, [(i, (i + k) % n) for i in range(n)])]
  transfers between devices with their start and end apart: 14 -> 34, of which waited for: 12 -> 10; matrix products, arithmetic and copies ran while one was open for 8% -> 8% of each run, Pallas kernels for 0% -> 1%
where the time goes in v2:
time: 216 us; the launch traced here: 215 us
  waiting for transfers between devices  83.9 us (39%)
  starting transfers between devices  59.3 us (27%)
  Pallas kernels  33.6 us (16%)
  local copies, waits for them, and re-layouts  25.6 us (12%)
  other arithmetic  7.32 us (3%)
  matrix products  3.25 us (2%)
    ppermute x30, waiting for transfers between devices, shift(): return lax.ppermute(v, axis, [(i, (i + k) % n) for i in range(n)])  61.2 us
    ppermute x30, starting transfers between devices, shift(): return lax.ppermute(v, axis, [(i, (i + k) % n) for i in range(n)])  32.5 us
    pallas_call x2, Pallas kernels, decode(): pl.pallas_call(functools.partial(decode_kernel, head is not None, m, widt...  31.5 us
    all_to_all x4, starting transfers between devices, exchange(): return lax.all_to_all(v, axis, 0, 0, tiled=True)  26.8 us
    all_to_all x4, waiting for transfers between devices, exchange(): return lax.all_to_all(v, axis, 0, 0, tiled=True)  22.7 us
    unnamed x63, local copies, waits for them, and re-layouts  18.1 us
  transfers between devices with their start and end apart: 34, of which 10 were waited for; matrix products, arithmetic and copies ran while one was open for 8% of the time, Pallas kernels for 1%

profile of v2, /device:TPU:1, one launch (start us, length us, event | category | flops | bytes accessed | tf_op | source)
XLA Modules:
  0.0 214.7 jit_solution(464199561057690540)
XLA Ops:
  0.6 2.2 %copy-done = f32[1,2048,512]{2,1,0:T(8,128)S(1)} copy-done((f32[1,2048,512]{2,1,0:T(8,128)S(1)}, f32[1,2048,512]{2,1,0:T(8,128)}, u32[]{:S(2)}) %copy-start) | copy-done | bytes 4194328
  3.2 3.3 %collective-permute-start = (bf16[4,8,32,512]{3,2,1,0:T(8,128)(2,1)S(1)}, bf16[4,8,32,512]{3,2,1,0:T(8,128)(2,1)S(1)}, u32[]{:S(2)}, u32[]{:S(2)}) collective-permute-start(bf16[4,8,32,512]{3,2,1,0:T(8,128)(2,1)S(1)} %shard_map.146), channel_id=1, source_target_pairs={{0,4},{4,0},{1,5},{5,1},{2,6},{6,2},{3,7},{7,3},{8,12},{12,8},{9,1... | collective-permute-start | bytes 3145736 | tf_op jit(solution)/shard_map/ppermute | solution.py:33
  7.5 2.2 %collective-permute-start.2 = (bf16[2048,64]{1,0:T(8,128)(2,1)}, bf16[2048,64]{1,0:T(8,128)(2,1)}, u32[]{:S(2)}, u32[]{:S(2)}) collective-permute-start(bf16[2048,64]{1,0:T(8,128)(2,1)} %copy.53), channel_id=1, source_target_pairs={{0,2},{1,3},{2,0},{3,1},{4,6},{5,7},{6,4},{7,5},{8,10},{9,11},{10,... | collective-permute-start | bytes 786440 | tf_op jit(solution)/shard_map/ppermute | solution.py:33
  12.7 2.2 %copy-done.1 = f32[1,2048,512]{2,1,0:T(8,128)S(1)} copy-done((f32[1,2048,512]{2,1,0:T(8,128)S(1)}, f32[1,2048,512]{2,1,0:T(8,128)}, u32[]{:S(2)}) %copy-start.1) | copy-done | bytes 4194328
  14.9 1.7 shard_map.147
  16.6 4.1 %all-to-all-start = ((bf16[4,8,32,512]{3,2,1,0:T(8,128)(2,1)}), bf16[4,8,32,512]{3,2,1,0:T(8,128)(2,1)S(1)}, u32[]{:S(2)}, u32[]{:S(2)}) async-start(bf16[4,8,32,512]{3,2,1,0:T(8,128)(2,1)} %shard_map.147), calls=%async_computation | async-start | bytes 2097152 | tf_op jit(solution)/shard_map/all_to_all | solution.py:27
  21.4 12.9 %all-to-all-done = bf16[4,8,32,512]{3,2,1,0:T(8,128)(2,1)S(1)} async-done(((bf16[4,8,32,512]{3,2,1,0:T(8,128)(2,1)}), bf16[4,8,32,512]{3,2,1,0:T(8,128)(2,1)S(1)}, u32[]{:S(2)}, u32[]{:S(2)}) %all-to-all-start) | async-done | bytes 1048608 | tf_op jit(solution)/shard_map/all_to_all | solution.py:27
  35.2 8.2 %all-to-all-start.1 = ((bf16[8,32,512]{2,1,0:T(8,128)(2,1)}), bf16[8,32,512]{2,1,0:T(8,128)(2,1)S(1)}, u32[]{:S(2)}, u32[]{:S(2)}) async-start(bf16[8,32,512]{2,1,0:T(8,128)(2,1)} %reduce_sum.30), calls=%async_computation.1 | async-start | bytes 524288 | tf_op jit(solution)/shard_map/all_to_all | solution.py:27
  43.4 1.6 convolution_convert_fusion
  44.9 3.3 %reshape.112 = bf16[64,3,2176]{2,1,0:T(4,128)(2,1)} reshape(bf16[192,2176]{1,0:T(8,128)(2,1)} %convolution_convert_fusion) | data formatting | bytes 1671168 | tf_op jit(solution)/shard_map/reshape | solution.py:211
  48.3 1.8 fusion.2
  50.1 2.7 %all-to-all-done.1 = bf16[8,32,512]{2,1,0:T(8,128)(2,1)S(1)} async-done(((bf16[8,32,512]{2,1,0:T(8,128)(2,1)}), bf16[8,32,512]{2,1,0:T(8,128)(2,1)S(1)}, u32[]{:S(2)}, u32[]{:S(2)}) %all-to-all-start.1) | async-done | bytes 262176 | tf_op jit(solution)/shard_map/all_to_all | solution.py:27
  54.3 4.0 %all-to-all-start.2 = ((bf16[8,32,512]{2,1,0:T(8,128)(2,1)}), bf16[8,32,512]{2,1,0:T(8,128)(2,1)S(1)}, u32[]{:S(2)}, u32[]{:S(2)}) async-start(bf16[8,32,512]{2,1,0:T(8,128)(2,1)} %broadcast_in_dim.15), calls=%async_computation.2 | async-start | bytes 524288 | tf_op jit(solution)/shard_map/all_to_all | solution.py:27
  58.3 2.2 %pad_maximum_fusion.refs_0_ = bf16[2048,256]{1,0:T(8,128)(2,1)S(1)} fusion(bf16[2048,64]{1,0:T(8,128)(2,1)} %collective-permute-done.3, bf16[2048,64]{1,0:T(8,128)(2,1)} %collective-permute-done.2, bf16[2048,64]{1,0:T(8,128)(2,1)} %collective-permute-done.1, bf16[2048,64]{1,0:T(8,128)(2,1)} %copy.53), kind=kLoop, calls=%fused_computation.8 | loop fusion | flops 4194304 | bytes 2097152 | tf_op jit(solution)/shard_map/concatenate | solution.py:196
  60.5 7.2 %all-to-all-done.2 = bf16[8,32,512]{2,1,0:T(8,128)(2,1)S(1)} async-done(((bf16[8,32,512]{2,1,0:T(8,128)(2,1)}), bf16[8,32,512]{2,1,0:T(8,128)(2,1)S(1)}, u32[]{:S(2)}, u32[]{:S(2)}) %all-to-all-start.2) | async-done | bytes 262176 | tf_op jit(solution)/shard_map/all_to_all | solution.py:27
  70.0 10.5 %all-to-all-start.3 = ((bf16[64,3,2176]{2,1,0:T(4,128)(2,1)}), bf16[64,3,2176]{2,1,0:T(4,128)(2,1)}, u32[]{:S(2)}, u32[]{:S(2)}) async-start(bf16[64,3,2176]{2,1,0:T(4,128)(2,1)} %reshape.112), calls=%async_computation.3 | async-start | bytes 2228224 | tf_op jit(solution)/shard_map/all_to_all | solution.py:27
  82.7 1.6 collective-permute-start.12
  85.1 25.5 %collective-permute-done.16 = bf16[8,32,256]{2,1,0:T(8,128)(2,1)S(1)} collective-permute-done((bf16[8,32,256]{2,1,0:T(8,128)(2,1)S(1)}, bf16[8,32,256]{2,1,0:T(8,128)(2,1)S(1)}, u32[]{:S(2)}, u32[]{:S(2)}) %collective-permute-start.16) | collective-permute-done | bytes 131104 | tf_op jit(solution)/shard_map/ppermute | solution.py:33
  111.4 4.5 %collective-permute-done.15 = bf16[8,32,256]{2,1,0:T(8,128)(2,1)S(1)} collective-permute-done((bf16[8,32,256]{2,1,0:T(8,128)(2,1)S(1)}, bf16[8,32,256]{2,1,0:T(8,128)(2,1)S(1)}, u32[]{:S(2)}, u32[]{:S(2)}) %collective-permute-start.15) | collective-permute-done | bytes 131104 | tf_op jit(solution)/shard_map/ppermute | solution.py:33
  117.3 4.0 %collective-permute-done.14 = bf16[8,32,256]{2,1,0:T(8,128)(2,1)S(1)} collective-permute-done((bf16[8,32,256]{2,1,0:T(8,128)(2,1)S(1)}, bf16[8,32,256]{2,1,0:T(8,128)(2,1)S(1)}, u32[]{:S(2)}, u32[]{:S(2)}) %collective-permute-start.14) | collective-permute-done | bytes 131104 | tf_op jit(solution)/shard_map/ppermute | solution.py:33
  121.5 3.1 %collective-permute-start.17 = (bf16[4,8,32,256]{3,2,1,0:T(8,128)(2,1)S(1)}, bf16[4,8,32,256]{3,2,1,0:T(8,128)(2,1)S(1)}, u32[]{:S(2)}, u32[]{:S(2)}) collective-permute-start(bf16[4,8,32,256]{3,2,1,0:T(8,128)(2,1)S(1)} %pad_maximum_fusion.2.refs_8_.refs_9_), channel_id=1, source_target_pairs={{0,4},{4,0},{1,5},{5,1},{2,6},{6,2},{3,7},{7,3},{8,12},{12,8},{9,1... | collective-permute-start | bytes 1572872 | tf_op jit(solution)/shard_map/ppermute | solution.py:33
  126.3 2.4 %collective-permute-start.20 = (bf16[4,8,32,256]{3,2,1,0:T(8,128)(2,1)S(1)}, bf16[4,8,32,256]{3,2,1,0:T(8,128)(2,1)}, u32[]{:S(2)}, u32[]{:S(2)}) collective-permute-start(bf16[4,8,32,256]{3,2,1,0:T(8,128)(2,1)S(1)} %pad_maximum_fusion.2.refs_8_.refs_9_), channel_id=1, source_target_pairs={{0,16},{8,24},{16,0},{24,8},{1,17},{9,25},{17,1},{25,9},{2,18},{10... | collective-permute-start | bytes 1572872 | tf_op jit(solution)/shard_map/ppermute | solution.py:33
  133.2 6.8 %collective-permute-done.18.refs_10_.refs_11_ = bf16[4,8,32,256]{3,2,1,0:T(8,128)(2,1)S(1)} collective-permute-done((bf16[4,8,32,256]{3,2,1,0:T(8,128)(2,1)S(1)}, bf16[4,8,32,256]{3,2,1,0:T(8,128)(2,1)S(1)}, u32[]{:S(2)}, u32[]{:S(2)}) %collective-permute-start.18) | collective-permute-done | bytes 524320 | tf_op jit(solution)/shard_map/ppermute | solution.py:33
  140.9 11.2 %collective-permute-done.20.refs_12_.refs_13_ = bf16[4,8,32,256]{3,2,1,0:T(8,128)(2,1)} collective-permute-done((bf16[4,8,32,256]{3,2,1,0:T(8,128)(2,1)S(1)}, bf16[4,8,32,256]{3,2,1,0:T(8,128)(2,1)}, u32[]{:S(2)}, u32[]{:S(2)}) %collective-permute-start.20) | collective-permute-done | bytes 524320 | tf_op jit(solution)/shard_map/ppermute | solution.py:33
  154.4 2.5 %reshape.113.rows_ref = bf16[192,2176]{1,0:T(8,128)(2,1)S(1)} reshape(bf16[64,3,2176]{2,1,0:T(4,128)(2,1)} %all-to-all-done.3) | data formatting | bytes 1671168 | tf_op jit(solution)/shard_map/reshape | solution.py:230
  165.4 17.1 %shard_map.148 = bf16[4,192,512]{2,1,0:T(8,128)(2,1)S(1)} custom-call(s32[4]{0:T(128)S(1)} %pad_add_fusion.place, bf16[192,2176]{1,0:T(8,128)(2,1)S(1)} %reshape.113.rows_ref, bf16[256,2048]{1,0:T(8,128)(2,1)S(1)} %copy-done.8, f32[1,2048]{1,0:T(1,128)S(1)} %bitcast.51, bf16[4,8,32,256]{3,2,1,0:T(8,128)(2,1)S(1)} %copy-done.3, ...), custom_call_target="tpu_custom_call" | custom-call | flops 6442450944 | bytes 8388608 | tf_op jit(solution)/shard_map/pallas_call | solution.py:144
  182.6 14.4 %shard_map.149 = f32[128,256]{1,0:T(8,128)S(1)} custom-call(s32[4]{0:T(128)S(1)} %pad_add_fusion.place, bf16[128,2176]{1,0:T(8,128)(2,1)S(1)} %constant_dynamic-slice_fusion.rows_ref, bf16[256,2048]{1,0:T(8,128)(2,1)S(1)} %copy-done.8, f32[1,2048]{1,0:T(1,128)S(1)} %bitcast.52, bf16[2048,256]{1,0:T(8,128)(2,1)S(1)} %pad_maximum_fusion.refs_0_, ...), custom_call_target="tpu_custom_call" | custom-call | flops 4294967296 | bytes 8388608 | tf_op jit(solution)/shard_map/pallas_call | solution.py:144
  197.3 2.4 %collective-permute-start.25 = (f32[128,64]{1,0:T(8,128)S(1)}, f32[128,64]{1,0:T(8,128)S(1)}, u32[]{:S(2)}, u32[]{:S(2)}) collective-permute-start(f32[128,64]{1,0:T(8,128)S(1)} %get-tuple-element.30), channel_id=1, source_target_pairs={{0,2},{1,3},{2,0},{3,1},{4,6},{5,7},{6,4},{7,5},{8,10},{9,11},{10,... | collective-permute-start | bytes 98312 | tf_op jit(solution)/shard_map/ppermute | solution.py:33
  201.0 2.3 %collective-permute-start.28 = (bf16[192,512]{1,0:T(8,128)(2,1)S(1)}, bf16[192,512]{1,0:T(8,128)(2,1)S(1)}, u32[]{:S(2)}, u32[]{:S(2)}) collective-permute-start(bf16[192,512]{1,0:T(8,128)(2,1)S(1)} %get-tuple-element.23), channel_id=1, source_target_pairs={{0,2},{1,3},{2,0},{3,1},{4,6},{5,7},{6,4},{7,5},{8,10},{9,11},{10,... | collective-permute-start | bytes 589832 | tf_op jit(solution)/shard_map/ppermute | solution.py:33
  204.0 4.1 %collective-permute-done.29 = bf16[192,512]{1,0:T(8,128)(2,1)S(1)} collective-permute-done((bf16[192,512]{1,0:T(8,128)(2,1)S(1)}, bf16[192,512]{1,0:T(8,128)(2,1)S(1)}, u32[]{:S(2)}, u32[]{:S(2)}) %collective-permute-start.29) | collective-permute-done | bytes 196640 | tf_op jit(solution)/shard_map/ppermute | solution.py:33
  208.1 4.9 %collective-permute-done.27 = bf16[192,512]{1,0:T(8,128)(2,1)S(1)} collective-permute-done((bf16[192,512]{1,0:T(8,128)(2,1)S(1)}, bf16[192,512]{1,0:T(8,128)(2,1)S(1)}, u32[]{:S(2)}, u32[]{:S(2)}) %collective-permute-start.27) | collective-permute-done | bytes 196640 | tf_op jit(solution)/shard_map/ppermute | solution.py:33
  213.0 1.7 fusion.3
  (141 shorter events, 34.4 us)
Async XLA Ops:
  3.2 9.5 %collective-permute-start = (bf16[4,8,32,512]{3,2,1,0:T(8,128)(2,1)S(1)}, bf16[4,8,32,512]{3,2,1,0:T(8,128)(2,1)S(1)}, u32[]{:S(2)}, u32[]{:S(2)}) collective-permute-start(bf16[4,8,32,512]{3,2,1,0:T(8,128)(2,1)S(1)} %shard_map.146), channel_id=1, source_target_pairs={{0,4},{4,0},{1,5},{5,1},{2,6},{6,2},{3,7},{7,3},{8,12},{12,8},{9,1... | collective-permute-start | bytes 3145736 | tf_op jit(solution)/shard_map/ppermute | solution.py:33
  7.5 50.8 %collective-permute-start.3 = (bf16[2048,64]{1,0:T(8,128)(2,1)}, bf16[2048,64]{1,0:T(8,128)(2,1)}, u32[]{:S(2)}, u32[]{:S(2)}) collective-permute-start(bf16[2048,64]{1,0:T(8,128)(2,1)} %copy.53), channel_id=1, source_target_pairs={{0,1},{1,2},{2,3},{3,0},{4,5},{5,6},{6,7},{7,4},{8,9},{9,10},{10,1... | collective-permute-start | bytes 786440 | tf_op jit(solution)/shard_map/ppermute | solution.py:33
  7.5 50.8 %collective-permute-start.2 = (bf16[2048,64]{1,0:T(8,128)(2,1)}, bf16[2048,64]{1,0:T(8,128)(2,1)}, u32[]{:S(2)}, u32[]{:S(2)}) collective-permute-start(bf16[2048,64]{1,0:T(8,128)(2,1)} %copy.53), channel_id=1, source_target_pairs={{0,2},{1,3},{2,0},{3,1},{4,6},{5,7},{6,4},{7,5},{8,10},{9,11},{10,... | collective-permute-start | bytes 786440 | tf_op jit(solution)/shard_map/ppermute | solution.py:33
  9.7 48.6 %collective-permute-start.1 = (bf16[2048,64]{1,0:T(8,128)(2,1)}, bf16[2048,64]{1,0:T(8,128)(2,1)}, u32[]{:S(2)}, u32[]{:S(2)}) collective-permute-start(bf16[2048,64]{1,0:T(8,128)(2,1)} %copy.53), channel_id=1, source_target_pairs={{0,3},{1,0},{2,1},{3,2},{4,7},{5,4},{6,5},{7,6},{8,11},{9,8},{10,9... | collective-permute-start | bytes 786440 | tf_op jit(solution)/shard_map/ppermute | solution.py:33
  16.6 17.6 %all-to-all-start = ((bf16[4,8,32,512]{3,2,1,0:T(8,128)(2,1)}), bf16[4,8,32,512]{3,2,1,0:T(8,128)(2,1)S(1)}, u32[]{:S(2)}, u32[]{:S(2)}) async-start(bf16[4,8,32,512]{3,2,1,0:T(8,128)(2,1)} %shard_map.147), calls=%async_computation | async-start | bytes 2097152 | tf_op jit(solution)/shard_map/all_to_all | solution.py:27
  35.2 17.6 %all-to-all-start.1 = ((bf16[8,32,512]{2,1,0:T(8,128)(2,1)}), bf16[8,32,512]{2,1,0:T(8,128)(2,1)S(1)}, u32[]{:S(2)}, u32[]{:S(2)}) async-start(bf16[8,32,512]{2,1,0:T(8,128)(2,1)} %reduce_sum.30), calls=%async_computation.1 | async-start | bytes 524288 | tf_op jit(solution)/shard_map/all_to_all | solution.py:27
  54.3 13.4 %all-to-all-start.2 = ((bf16[8,32,512]{2,1,0:T(8,128)(2,1)}), bf16[8,32,512]{2,1,0:T(8,128)(2,1)S(1)}, u32[]{:S(2)}, u32[]{:S(2)}) async-start(bf16[8,32,512]{2,1,0:T(8,128)(2,1)} %broadcast_in_dim.15), calls=%async_computation.2 | async-start | bytes 524288 | tf_op jit(solution)/shard_map/all_to_all | solution.py:27
  67.7 12.7 %collective-permute-start.6 = (bf16[8,32,256]{2,1,0:T(8,128)(2,1)S(1)}, bf16[8,32,256]{2,1,0:T(8,128)(2,1)S(1)}, u32[]{:S(2)}, u32[]{:S(2)}) collective-permute-start(bf16[8,32,256]{2,1,0:T(8,128)(2,1)S(1)} %get-tuple-element.28), channel_id=1, source_target_pairs={{0,24},{8,0},{16,8},{24,16},{1,25},{9,1},{17,9},{25,17},{2,26},{10... | collective-permute-start | bytes 393224 | tf_op jit(solution)/shard_map/ppermute | solution.py:33
  68.8 11.7 %collective-permute-start.5 = (bf16[8,32,256]{2,1,0:T(8,128)(2,1)S(1)}, bf16[8,32,256]{2,1,0:T(8,128)(2,1)S(1)}, u32[]{:S(2)}, u32[]{:S(2)}) collective-permute-start(bf16[8,32,256]{2,1,0:T(8,128)(2,1)S(1)} %get-tuple-element.28), channel_id=1, source_target_pairs={{0,16},{8,24},{16,0},{24,8},{1,17},{9,25},{17,1},{25,9},{2,18},{10... | collective-permute-start | bytes 393224 | tf_op jit(solution)/shard_map/ppermute | solution.py:33
  70.0 10.5 %collective-permute-start.4 = (bf16[8,32,256]{2,1,0:T(8,128)(2,1)S(1)}, bf16[8,32,256]{2,1,0:T(8,128)(2,1)S(1)}, u32[]{:S(2)}, u32[]{:S(2)}) collective-permute-start(bf16[8,32,256]{2,1,0:T(8,128)(2,1)S(1)} %get-tuple-element.28), channel_id=1, source_target_pairs={{0,8},{8,16},{16,24},{24,0},{1,9},{9,17},{17,25},{25,1},{2,10},{10... | collective-permute-start | bytes 393224 | tf_op jit(solution)/shard_map/ppermute | solution.py:33
  70.0 84.4 %all-to-all-start.3 = ((bf16[64,3,2176]{2,1,0:T(4,128)(2,1)}), bf16[64,3,2176]{2,1,0:T(4,128)(2,1)}, u32[]{:S(2)}, u32[]{:S(2)}) async-start(bf16[64,3,2176]{2,1,0:T(4,128)(2,1)} %reshape.112), calls=%async_computation.3 | async-start | bytes 2228224 | tf_op jit(solution)/shard_map/all_to_all | solution.py:27
  80.6 43.9 %collective-permute-start.7 = (bf16[4,8,32,256]{3,2,1,0:T(8,128)(2,1)S(1)}, bf16[4,8,32,256]{3,2,1,0:T(8,128)(2,1)S(1)}, u32[]{:S(2)}, u32[]{:S(2)}) collective-permute-start(bf16[4,8,32,256]{3,2,1,0:T(8,128)(2,1)S(1)} %pad_maximum_fusion.1.refs_0_.refs_1_), channel_id=1, source_target_pairs={{0,4},{4,0},{1,5},{5,1},{2,6},{6,2},{3,7},{7,3},{8,12},{12,8},{9,1... | collective-permute-start | bytes 1572872 | tf_op jit(solution)/shard_map/ppermute | solution.py:33
  81.5 44.8 %collective-permute-start.8 = (bf16[4,8,32,256]{3,2,1,0:T(8,128)(2,1)S(1)}, bf16[4,8,32,256]{3,2,1,0:T(8,128)(2,1)S(1)}, u32[]{:S(2)}, u32[]{:S(2)}) collective-permute-start(bf16[4,8,32,256]{3,2,1,0:T(8,128)(2,1)S(1)} %pad_maximum_fusion.1.refs_0_.refs_1_), channel_id=1, source_target_pairs={{0,1},{1,2},{2,3},{3,0},{4,5},{5,6},{6,7},{7,4},{8,9},{9,10},{10,1... | collective-permute-start | bytes 1572872 | tf_op jit(solution)/shard_map/ppermute | solution.py:33
  81.9 46.8 %collective-permute-start.10 = (bf16[4,8,32,256]{3,2,1,0:T(8,128)(2,1)S(1)}, bf16[4,8,32,256]{3,2,1,0:T(8,128)(2,1)}, u32[]{:S(2)}, u32[]{:S(2)}) collective-permute-start(bf16[4,8,32,256]{3,2,1,0:T(8,128)(2,1)S(1)} %pad_maximum_fusion.1.refs_0_.refs_1_), channel_id=1, source_target_pairs={{0,2},{1,3},{2,0},{3,1},{4,6},{5,7},{6,4},{7,5},{8,10},{9,11},{10,... | collective-permute-start | bytes 1572872 | tf_op jit(solution)/shard_map/ppermute | solution.py:33
  82.7 48.0 %collective-permute-start.12 = (bf16[4,8,32,256]{3,2,1,0:T(8,128)(2,1)S(1)}, bf16[4,8,32,256]{3,2,1,0:T(8,128)(2,1)}, u32[]{:S(2)}, u32[]{:S(2)}) collective-permute-start(bf16[4,8,32,256]{3,2,1,0:T(8,128)(2,1)S(1)} %pad_maximum_fusion.1.refs_0_.refs_1_), channel_id=1, source_target_pairs={{0,3},{1,0},{2,1},{3,2},{4,7},{5,4},{6,5},{7,6},{8,11},{9,8},{10,9... | collective-permute-start | bytes 1572872 | tf_op jit(solution)/shard_map/ppermute | solution.py:33
  84.3 26.4 %collective-permute-start.16 = (bf16[8,32,256]{2,1,0:T(8,128)(2,1)S(1)}, bf16[8,32,256]{2,1,0:T(8,128)(2,1)S(1)}, u32[]{:S(2)}, u32[]{:S(2)}) collective-permute-start(bf16[8,32,256]{2,1,0:T(8,128)(2,1)S(1)} %get-tuple-element.27), channel_id=1, source_target_pairs={{0,3},{1,0},{2,1},{3,2},{4,7},{5,4},{6,5},{7,6},{8,11},{9,8},{10,9... | collective-permute-start | bytes 393224 | tf_op jit(solution)/shard_map/ppermute | solution.py:33
  110.6 5.3 %collective-permute-start.15 = (bf16[8,32,256]{2,1,0:T(8,128)(2,1)S(1)}, bf16[8,32,256]{2,1,0:T(8,128)(2,1)S(1)}, u32[]{:S(2)}, u32[]{:S(2)}) collective-permute-start(bf16[8,32,256]{2,1,0:T(8,128)(2,1)S(1)} %get-tuple-element.27), channel_id=1, source_target_pairs={{0,2},{1,3},{2,0},{3,1},{4,6},{5,7},{6,4},{7,5},{8,10},{9,11},{10,... | collective-permute-start | bytes 393224 | tf_op jit(solution)/shard_map/ppermute | solution.py:33
  115.9 5.4 %collective-permute-start.14 = (bf16[8,32,256]{2,1,0:T(8,128)(2,1)S(1)}, bf16[8,32,256]{2,1,0:T(8,128)(2,1)S(1)}, u32[]{:S(2)}, u32[]{:S(2)}) collective-permute-start(bf16[8,32,256]{2,1,0:T(8,128)(2,1)S(1)} %get-tuple-element.27), channel_id=1, source_target_pairs={{0,1},{1,2},{2,3},{3,0},{4,5},{5,6},{6,7},{7,4},{8,9},{9,10},{10,1... | collective-permute-start | bytes 393224 | tf_op jit(solution)/shard_map/ppermute | solution.py:33
  121.5 10.9 %collective-permute-start.17 = (bf16[4,8,32,256]{3,2,1,0:T(8,128)(2,1)S(1)}, bf16[4,8,32,256]{3,2,1,0:T(8,128)(2,1)S(1)}, u32[]{:S(2)}, u32[]{:S(2)}) collective-permute-start(bf16[4,8,32,256]{3,2,1,0:T(8,128)(2,1)S(1)} %pad_maximum_fusion.2.refs_8_.refs_9_), channel_id=1, source_target_pairs={{0,4},{4,0},{1,5},{5,1},{2,6},{6,2},{3,7},{7,3},{8,12},{12,8},{9,1... | collective-permute-start | bytes 1572872 | tf_op jit(solution)/shard_map/ppermute | solution.py:33
  125.3 14.7 %collective-permute-start.18 = (bf16[4,8,32,256]{3,2,1,0:T(8,128)(2,1)S(1)}, bf16[4,8,32,256]{3,2,1,0:T(8,128)(2,1)S(1)}, u32[]{:S(2)}, u32[]{:S(2)}) collective-permute-start(bf16[4,8,32,256]{3,2,1,0:T(8,128)(2,1)S(1)} %pad_maximum_fusion.2.refs_8_.refs_9_), channel_id=1, source_target_pairs={{0,8},{8,16},{16,24},{24,0},{1,9},{9,17},{17,25},{25,1},{2,10},{10... | collective-permute-start | bytes 1572872 | tf_op jit(solution)/shard_map/ppermute | solution.py:33
  126.3 25.8 %collective-permute-start.20 = (bf16[4,8,32,256]{3,2,1,0:T(8,128)(2,1)S(1)}, bf16[4,8,32,256]{3,2,1,0:T(8,128)(2,1)}, u32[]{:S(2)}, u32[]{:S(2)}) collective-permute-start(bf16[4,8,32,256]{3,2,1,0:T(8,128)(2,1)S(1)} %pad_maximum_fusion.2.refs_8_.refs_9_), channel_id=1, source_target_pairs={{0,16},{8,24},{16,0},{24,8},{1,17},{9,25},{17,1},{25,9},{2,18},{10... | collective-permute-start | bytes 1572872 | tf_op jit(solution)/shard_map/ppermute | solution.py:33
  128.7 24.2 %collective-permute-start.22 = (bf16[4,8,32,256]{3,2,1,0:T(8,128)(2,1)S(1)}, bf16[4,8,32,256]{3,2,1,0:T(8,128)(2,1)}, u32[]{:S(2)}, u32[]{:S(2)}) collective-permute-start(bf16[4,8,32,256]{3,2,1,0:T(8,128)(2,1)S(1)} %pad_maximum_fusion.2.refs_8_.refs_9_), channel_id=1, source_target_pairs={{0,24},{8,0},{16,8},{24,16},{1,25},{9,1},{17,9},{25,17},{2,26},{10... | collective-permute-start | bytes 1572872 | tf_op jit(solution)/shard_map/ppermute | solution.py:33
  130.7 22.2 %collective-permute-start.9 = (bf16[4,8,32,256]{3,2,1,0:T(8,128)(2,1)S(1)}, bf16[4,8,32,256]{3,2,1,0:T(8,128)(2,1)S(1)}, u32[]{:S(2)}, u32[]{:S(2)}) collective-permute-start(bf16[4,8,32,256]{3,2,1,0:T(8,128)(2,1)S(1)} %collective-permute-done.8.refs_2_.refs_3_), channel_id=1, source_target_pairs={{0,4},{4,0},{1,5},{5,1},{2,6},{6,2},{3,7},{7,3},{8,12},{12,8},{9,1... | collective-permute-start | bytes 1572872 | tf_op jit(solution)/shard_map/ppermute | solution.py:33
  133.2 23.6 %collective-permute-start.11 = (bf16[4,8,32,256]{3,2,1,0:T(8,128)(2,1)}, bf16[4,8,32,256]{3,2,1,0:T(8,128)(2,1)}, u32[]{:S(2)}, u32[]{:S(2)}) collective-permute-start(bf16[4,8,32,256]{3,2,1,0:T(8,128)(2,1)} %collective-permute-done.10.refs_4_.refs_5_), channel_id=1, source_target_pairs={{0,4},{4,0},{1,5},{5,1},{2,6},{6,2},{3,7},{7,3},{8,12},{12,8},{9,1... | collective-permute-start | bytes 1572872 | tf_op jit(solution)/shard_map/ppermute | solution.py:33
  140.1 16.8 %collective-permute-start.13 = (bf16[4,8,32,256]{3,2,1,0:T(8,128)(2,1)}, bf16[4,8,32,256]{3,2,1,0:T(8,128)(2,1)}, u32[]{:S(2)}, u32[]{:S(2)}) collective-permute-start(bf16[4,8,32,256]{3,2,1,0:T(8,128)(2,1)} %collective-permute-done.12.refs_6_.refs_7_), channel_id=1, source_target_pairs={{0,4},{4,0},{1,5},{5,1},{2,6},{6,2},{3,7},{7,3},{8,12},{12,8},{9,1... | collective-permute-start | bytes 1572872 | tf_op jit(solution)/shard_map/ppermute | solution.py:33
  152.1 4.8 %collective-permute-start.19 = (bf16[4,8,32,256]{3,2,1,0:T(8,128)(2,1)S(1)}, bf16[4,8,32,256]{3,2,1,0:T(8,128)(2,1)}, u32[]{:S(2)}, u32[]{:S(2)}) collective-permute-start(bf16[4,8,32,256]{3,2,1,0:T(8,128)(2,1)S(1)} %collective-permute-done.18.refs_10_.refs_11_), channel_id=1, source_target_pairs={{0,4},{4,0},{1,5},{5,1},{2,6},{6,2},{3,7},{7,3},{8,12},{12,8},{9,1... | collective-permute-start | bytes 1572872 | tf_op jit(solution)/shard_map/ppermute | solution.py:33
  197.2 6.2 %collective-permute-start.24 = (f32[128,64]{1,0:T(8,128)S(1)}, f32[128,64]{1,0:T(8,128)S(1)}, u32[]{:S(2)}, u32[]{:S(2)}) collective-permute-start(f32[128,64]{1,0:T(8,128)S(1)} %get-tuple-element.31), channel_id=1, source_target_pairs={{0,1},{1,2},{2,3},{3,0},{4,5},{5,6},{6,7},{7,4},{8,9},{9,10},{10,1... | collective-permute-start | bytes 98312 | tf_op jit(solution)/shard_map/ppermute | solution.py:33
  197.3 6.5 %collective-permute-start.25 = (f32[128,64]{1,0:T(8,128)S(1)}, f32[128,64]{1,0:T(8,128)S(1)}, u32[]{:S(2)}, u32[]{:S(2)}) collective-permute-start(f32[128,64]{1,0:T(8,128)S(1)} %get-tuple-element.30), channel_id=1, source_target_pairs={{0,2},{1,3},{2,0},{3,1},{4,6},{5,7},{6,4},{7,5},{8,10},{9,11},{10,... | collective-permute-start | bytes 98312 | tf_op jit(solution)/shard_map/ppermute | solution.py:33
  199.7 4.2 %collective-permute-start.26 = (f32[128,64]{1,0:T(8,128)S(1)}, f32[128,64]{1,0:T(8,128)S(1)}, u32[]{:S(2)}, u32[]{:S(2)}) collective-permute-start(f32[128,64]{1,0:T(8,128)S(1)} %get-tuple-element.29), channel_id=1, source_target_pairs={{0,3},{1,0},{2,1},{3,2},{4,7},{5,4},{6,5},{7,6},{8,11},{9,8},{10,9... | collective-permute-start | bytes 98312 | tf_op jit(solution)/shard_map/ppermute | solution.py:33
  200.0 8.1 %collective-permute-start.29 = (bf16[192,512]{1,0:T(8,128)(2,1)S(1)}, bf16[192,512]{1,0:T(8,128)(2,1)S(1)}, u32[]{:S(2)}, u32[]{:S(2)}) collective-permute-start(bf16[192,512]{1,0:T(8,128)(2,1)S(1)} %get-tuple-element.22), channel_id=1, source_target_pairs={{0,3},{1,0},{2,1},{3,2},{4,7},{5,4},{6,5},{7,6},{8,11},{9,8},{10,9... | collective-permute-start | bytes 589832 | tf_op jit(solution)/shard_map/ppermute | solution.py:33
  201.0 7.1 %collective-permute-start.28 = (bf16[192,512]{1,0:T(8,128)(2,1)S(1)}, bf16[192,512]{1,0:T(8,128)(2,1)S(1)}, u32[]{:S(2)}, u32[]{:S(2)}) collective-permute-start(bf16[192,512]{1,0:T(8,128)(2,1)S(1)} %get-tuple-element.23), channel_id=1, source_target_pairs={{0,2},{1,3},{2,0},{3,1},{4,6},{5,7},{6,4},{7,5},{8,10},{9,11},{10,... | collective-permute-start | bytes 589832 | tf_op jit(solution)/shard_map/ppermute | solution.py:33
  203.4 9.6 %collective-permute-start.27 = (bf16[192,512]{1,0:T(8,128)(2,1)S(1)}, bf16[192,512]{1,0:T(8,128)(2,1)S(1)}, u32[]{:S(2)}, u32[]{:S(2)}) collective-permute-start(bf16[192,512]{1,0:T(8,128)(2,1)S(1)} %get-tuple-element.24), channel_id=1, source_target_pairs={{0,1},{1,2},{2,3},{3,0},{4,5},{5,6},{6,7},{7,4},{8,9},{9,10},{10,1... | collective-permute-start | bytes 589832 | tf_op jit(solution)/shard_map/ppermute | solution.py:33
  (33 other events, 344.9 us)

commit v3 on v2

v3 whole, which is shorter than its diff:
```python
import functools

import jax
import jax.numpy as jnp
from jax import lax
from jax.experimental import pallas as pl
from jax.experimental.pallas import tpu as pltpu
from jax.sharding import Mesh, PartitionSpec as P

STEPS = 4
NZ, NX, NC, NY = 8, 4, 2, 4
DP = ("z", "x", "c")
TAGS = 128
VMEM_LIMIT = 60 * 2**20

beta_one = 0.9
beta_two = 0.999
corr_one = 1.0 - 0.9**10
corr_two = 1.0 - 0.999**10
rate_lr = 0.01
adam_eps = 1e-08
norm_eps = 1e-06
F32 = jnp.float32
BF16 = jnp.bfloat16


def exchange(v, axis):
    return lax.all_to_all(v, axis, 0, 0, tiled=True)


def shift(v, axis, k, n):
    if k == 0:
        return v
    return lax.ppermute(v, axis, [(i, (i + k) % n) for i in range(n)])


def swap(v):
    return shift(v, "c", 1, NC)


def core_rows_kernel(add, core, g_ref, *refs):
    if add:
        got_ref, refs = refs[0], refs[1:]
    out_ref, part, got, done, in_sems, got_sems, out_sems = refs
    nx = part.shape[0]
    loads, extra, stores = [], [], []
    for i in range(nx):
        loads.append(pltpu.make_async_copy(g_ref.at[:, i, core[0]], part.at[i], in_sems.at[i]))
        loads[-1].start()
        if add:
            extra.append(pltpu.make_async_copy(got_ref.at[i], got.at[i], got_sems.at[i]))
            extra[-1].start()
    for i in range(nx):
        loads[i].wait()
        if add:
            extra[i].wait()
            done[i] = (part[i] + got[i].astype(F32)).astype(BF16)
        else:
            done[i] = part[i].astype(BF16)
        stores.append(pltpu.make_async_copy(done.at[i], out_ref.at[i], out_sems.at[i]))
        stores[-1].start()
    for store in stores:
        store.wait()


def core_rows(core, g, *got):
    nz, nx, _, rows, cols = g.shape
    hbm = pl.BlockSpec(memory_space=pl.ANY)
    return pl.pallas_call(
        functools.partial(core_rows_kernel, bool(got)),
        in_specs=[pl.BlockSpec(memory_space=pltpu.SMEM), hbm] + [hbm for _ in got],
        out_specs=hbm,
        out_shape=jax.ShapeDtypeStruct((nx, nz, rows, cols), BF16),
        scratch_shapes=[
            pltpu.VMEM((nx, nz, rows, cols), F32),
            pltpu.VMEM((nx, nz, rows, cols), BF16),
            pltpu.VMEM((nx, nz, rows, cols), BF16),
            pltpu.SemaphoreType.DMA((nx,)),
            pltpu.SemaphoreType.DMA((nx,)),
            pltpu.SemaphoreType.DMA((nx,)),
        ],
        compiler_params=pltpu.CompilerParams(vmem_limit_bytes=VMEM_LIMIT),
    )(core[None].astype(jnp.int32), g, *got)


def decode_kernel(width, place, slots_ref, envs_ref, table_ref, gain_ref, *refs):
    n_pieces = 4 * NY
    heads, refs = refs[:NY], refs[NY:]
    pieces, (out_ref, w_ref, hidden, mixed, state, sems) = refs[:n_pieces], refs[n_pieces:]
    my_x, my_c, my_y = place[0], place[1], place[2]
    blocks, wide = w_ref.shape[0], w_ref.shape[-1]
    slots, own = slots_ref.shape[0], envs_ref.shape[0]
    m = slots + own
    tail = out_ref.shape[1] - slots
    groups = ((slots_ref, slice(0, slots), slots), (envs_ref, slice(slots, m), own))
    copies = ([], [])
    for p in range(n_pieces):
        second, k, other = p // (2 * NY), p % (2 * NY) // 2, p % 2
        core = lax.rem(my_c + other, NC)
        for i in range(NX):
            x_off, y_off = (k, i) if second else (i, k)
            x = lax.rem(my_x - x_off + NX, NX)
            y = lax.rem(my_y - y_off + NY, NY)
            copy = pltpu.make_async_copy(
                pieces[p].at[i], w_ref.at[2 * y + second, :, x, core], sems.at[p * NX + i]
            )
            copy.start()
            copies[second].append(copy)

    actions = table_ref.shape[0]

    def onehot(step, ref, count):
        tag = ref[:, width + step : width + step + 1].astype(jnp.int32)
        number = lax.broadcasted_iota(jnp.int32, (count, actions), 1) + 1
        return jnp.where(tag == number, 1.0, 0.0).astype(BF16)

    def embed(step, n, old, ref, at, count):
        cols = slice(n * wide, (n + 1) * wide)
        embedded = jnp.dot(onehot(step, ref, count), table_ref[:, cols], preferred_element_type=F32)
        hidden[at, cols] = (old.astype(F32) + embedded).astype(BF16)

    for n in range(blocks):
        for ref, at, count in groups:
            embed(0, n, ref[:, n * wide : (n + 1) * wide], ref, at, count)
    for step in range(STEPS):
        total = jnp.zeros((m, 1), F32)
        for second in range(2):
            if step == 0:
                for copy in copies[second]:
                    copy.wait()

            def multiply(i, total):
                for pair in range(2):
                    n = 4 * i + 2 * pair + second
                    w = w_ref[n].reshape(width, wide)
                    got = jnp.dot(hidden[...], w, preferred_element_type=F32).astype(BF16)
                    mixed[:, pl.ds(pl.multiple_of(n * wide, wide), wide)] = got
                    got = got.astype(F32)
                    total = total + jnp.sum(got * got, axis=1, keepdims=True)
                return total

            total = lax.fori_loop(0, blocks // 4, multiply, total)
        inverse = lax.rsqrt(total * (1.0 / width) + norm_eps)
        for n in range(blocks):
            cols = slice(n * wide, (n + 1) * wide)
            for ref, at, count in groups:
                old = ref[:, cols] if step == 0 else state[at, cols]
                new = old.astype(F32) + gain_ref[:, cols] * mixed[at, cols].astype(F32) * inverse[at]
                new = new.astype(BF16)
                if step < STEPS - 1:
                    state[at, cols] = new
                    embed(step + 1, n, new, ref, at, count)
                elif ref is envs_ref:
                    state[at, cols] = new
                else:
                    out_ref[n // 2, :slots, n % 2 * wide : (n % 2 + 1) * wide] = new
    for k in range(NY):
        scores = lax.dot_general(
            state[slots:m, :],
            heads[k][...],
            (((1,), (1,)), ((), ())),
            preferred_element_type=F32,
        )
        row = my_y * own + lax.broadcasted_iota(jnp.int32, scores.shape, 0)
        scores = (scores * jnp.where(row < place[3], 1.0, 0.0)).astype(BF16)
        packed = [scores[i * tail : (i + 1) * tail] for i in range(own // tail)]
        out_ref[lax.rem(my_y + k, NY), slots:, :] = jnp.concatenate(packed, 1)


def decode(place, slot_rows, env_rows, table, gain, heads, pieces):
    slots, own, width = slot_rows.shape[0], env_rows.shape[0], table.shape[1]
    wide, m = width // NY // 2, slots + own
    tail = own * heads[0].shape[0] // (width // NY)
    vmem = pl.BlockSpec(memory_space=pltpu.VMEM)
    return pl.pallas_call(
        functools.partial(decode_kernel, width),
        in_specs=[pl.BlockSpec(memory_space=pltpu.SMEM)]
        + [vmem] * (4 + NY)
        + [pl.BlockSpec(memory_space=pl.ANY)] * len(pieces),
        out_specs=vmem,
        out_shape=jax.ShapeDtypeStruct((NY, slots + tail, width // NY), BF16),
        scratch_shapes=[
            pltpu.VMEM((2 * NY, NZ, NX, NC, width // (NZ * NX * NC), wide), BF16),
            pltpu.VMEM((m, width), BF16),
            pltpu.VMEM((m, width), BF16),
            pltpu.VMEM((m, width), BF16),
            pltpu.SemaphoreType.DMA((len(pieces) * NX,)),
        ],
        compiler_params=pltpu.CompilerParams(vmem_limit_bytes=VMEM_LIMIT),
        cost_estimate=pl.CostEstimate(
            flops=2 * STEPS * m * width * width, bytes_accessed=2 * width * width, transcendentals=0
        ),
    )(place, slot_rows, env_rows, table, gain, *heads, *pieces)


def body(
    grad_parts,
    master,
    moment_one,
    moment_two,
    states,
    action_ids,
    env_counts,
    owners,
    act_table,
    norm_gain,
    head,
):
    width, cols = grad_parts.shape[1:]
    rows = width // (NZ * NX * NC)
    half = cols // 2
    env_slots = states.shape[0]
    owner_num = NZ * NX * NC
    capacity = max(2, 3 * env_slots // (2 * owner_num))
    share = capacity // NY
    slots = owner_num * share
    own = env_slots // NY
    my_x, my_c, my_y = lax.axis_index("x"), lax.axis_index("c"), lax.axis_index("y")
    place = jnp.stack([my_x, my_c, my_y, env_counts[0]]).astype(jnp.int32)

    g = grad_parts[0].reshape(NZ, NX, NC, rows, cols)
    both = core_rows(my_c, g, swap(core_rows(1 - my_c, g)))
    both, head = lax.optimization_barrier((both, head))
    by_x = exchange(both, "x")
    heads = [shift(head.T, "y", (NY - k) % NY, NY) for k in range(NY)]
    by_x, heads, states = lax.optimization_barrier((by_x, heads, states))
    by_x = by_x.astype(F32).sum(0).astype(BF16)
    gradient = exchange(by_x, "z").astype(F32).sum(0)

    active = jnp.arange(env_slots, dtype=jnp.int32) < env_counts[0]
    target = owners[:, 0]
    marks = (
        (target[:, None] == jnp.arange(owner_num, dtype=jnp.int32)[None, :]) & active[:, None]
    ).astype(jnp.int32)
    ranked = jnp.cumsum(marks, axis=0) - marks
    slot_idx = jnp.sum(ranked * marks, axis=1)
    mine = active & (slot_idx // share == my_y)
    column = target // NC % NX
    ahead = lax.rem(column - my_x + NX, NX)
    group = target // (NC * NX) * NC + target % NC
    groups = NZ * NC
    index = jnp.where(mine, (ahead * groups + group - my_y) * share + slot_idx, -1)
    pick = (jnp.arange(slots, dtype=jnp.int32)[:, None] == index[None, :]).astype(BF16)
    tags = jnp.pad((action_ids + 1).astype(BF16), ((0, 0), (0, TAGS - STEPS)))
    tagged = jnp.concatenate([states, tags], 1)
    outgoing = jnp.dot(pick, tagged, preferred_element_type=F32).astype(BF16)
    span = groups * share
    outgoing = [shift(outgoing[k * span : (k + 1) * span], "x", k, NX) for k in range(NX)]
    deep = -(-NX * share // 16) * 16
    row = jnp.arange(groups * deep, dtype=jnp.int32)
    place_in, part = row % deep, row // deep
    from_row = place_in // share * span + part * share + place_in % share
    from_row = jnp.where(place_in < NX * share, from_row, -1)
    pick = (from_row[:, None] == jnp.arange(slots, dtype=jnp.int32)[None, :]).astype(BF16)
    outgoing = jnp.dot(pick, jnp.concatenate(outgoing, 0), preferred_element_type=F32)
    outgoing = outgoing.astype(BF16).reshape(groups, deep, width + TAGS)
    actor_rows = lax.dynamic_slice_in_dim(tagged, my_y * own, own, 0)

    m_new = beta_one * moment_one + (1.0 - beta_one) * gradient
    v_new = beta_two * moment_two + (1.0 - beta_two) * gradient * gradient
    w_new = master - rate_lr * (m_new / corr_one) / (jnp.sqrt(v_new / corr_two) + adam_eps)

    w = exchange(jnp.broadcast_to(w_new.astype(BF16)[None], (NZ, rows, cols)), "z")
    w, outgoing, actor_rows = lax.optimization_barrier((w, outgoing, actor_rows))
    first, second = w[..., :half], w[..., half:]
    first = jnp.stack([shift(first, "x", k, NX) for k in range(NX)])
    second = jnp.stack([shift(second, "y", k, NY) for k in range(NY)])
    arrived = exchange(outgoing, ("z", "c")).reshape(groups * deep, width + TAGS)
    row = jnp.arange(slots, dtype=jnp.int32)
    source, behind = row // share, lax.rem(my_x - row // share // NC % NX + NX, NX)
    from_row = (source // (NC * NX) * NC + source % NC) * deep + behind * share + row % share
    pick = (from_row[:, None] == jnp.arange(groups * deep, dtype=jnp.int32)[None, :]).astype(BF16)
    slot_rows = jnp.dot(pick, arrived, preferred_element_type=F32).astype(BF16)
    first, second = lax.optimization_barrier((first, second))
    moved = [shift(first, "y", k, NY) for k in range(1, NY)]
    moved += [shift(second, "x", k, NX) for k in range(1, NX)]
    moved, slot_rows = lax.optimization_barrier((moved, slot_rows))
    pieces = []
    for piece in [first, *moved[: NY - 1], second, *moved[NY - 1 :]]:
        pieces += [piece, swap(piece)]

    final = decode(place, slot_rows, actor_rows, act_table, norm_gain[None, :], heads, pieces)
    landed = exchange(final, "y")

    each = head.shape[1]
    scores = landed[:, slots:].astype(F32).reshape(NY, -1, cols // each, each)
    logits = jnp.transpose(scores, (0, 2, 1, 3)).reshape(env_slots, each)

    row = jnp.arange(owner_num * capacity, dtype=jnp.int32)
    at = row % capacity // share * slots + row // capacity * share + row % share
    order = (at[:, None] == row[None, :]).astype(BF16)
    landed = landed[:, :slots].reshape(owner_num * capacity, cols)
    received = jnp.dot(order, landed, preferred_element_type=F32)
    return (m_new, v_new, w_new, logits, received.astype(BF16))


def solution(mesh):
    grid = Mesh(mesh.devices.reshape(NZ, NX, NC, NY), DP + ("y",))
    in_specs = (
        P(DP, None, "y"),
        P(DP, "y"),
        P(DP, "y"),
        P(DP, "y"),
        P(DP, None),
        P(DP, None),
        P(DP),
        P(DP, None),
        P(),
        P(),
        P(None, "y"),
    )
    out_specs = (P(DP, "y"),) * 5
    return jax.shard_map(body, mesh=grid, in_specs=in_specs, out_specs=out_specs, check_vma=False)
```

time: 216 us -> 180 us (0.83)
  waiting for transfers between devices: 83.9 us -> 61.7 us
  local copies, waits for them, and re-layouts: 25.6 us -> 8.92 us
  starting transfers between devices: 59.3 us -> 65.8 us
  Pallas kernels: 33.6 us -> 30.3 us
  matrix products: 3.25 us -> 6.37 us
  other arithmetic: 7.32 us -> 4.97 us
    ppermute x30 -> x27, waiting for transfers between devices: 61.2 us -> 38.1 us  [shift(): return lax.ppermute(v, axis, [(i, (i + k) % n) for i in range(n)])]
    unnamed x63 -> x39, local copies, waits for them, and re-layouts: 18.1 us -> 5.93 us
    ppermute x30 -> x27, starting transfers between devices: 32.5 us -> 40 us  [shift(): return lax.ppermute(v, axis, [(i, (i + k) % n) for i in range(n)])]
    reshape x2, local copies, waits for them, and re-layouts: 5.78 us -> 0.15 us  [body(): logits = jnp.transpose(scores, (0, 2, 1, 3)).reshape(env_slots, each)]
    pallas_call x4 -> x3, Pallas kernels: 33.6 us -> 30.3 us  [the longest x1 25.3 us: decode(): pl.pallas_call(functools.partial(decode_kernel, width), in_specs=[pl.Bloc...]
    dot_general x2 -> x4, matrix products: 3.25 us -> 6.37 us  [the longest x1 2.67 us: body(): jnp.dot(pick, jnp.concatenate(outgoing, 0), preferred_element_type=F32)]
    concatenate x1 -> x0, other arithmetic: 2.19 us -> none  [body(): jnp.concatenate([shift(head, 'y', (NY - k) % NY, NY) for k in range(NY)], 1)]
    all_to_all x4 -> x5, starting transfers between devices: 26.8 us -> 25.8 us  [exchange(): return lax.all_to_all(v, axis, 0, 0, tiled=True)]
  transfers between devices with their start and end apart: 34 -> 32, of which waited for: 10 -> 16; matrix products, arithmetic and copies ran while one was open for 8% -> 6% of each run, Pallas kernels for 1% -> 0%
where the time goes in v3:
time: 180 us
  starting transfers between devices  65.8 us (37%)
  waiting for transfers between devices  61.7 us (34%)
  Pallas kernels  30.3 us (17%)
  local copies, waits for them, and re-layouts  8.92 us (5%)
  matrix products  6.37 us (4%)
  other arithmetic  4.97 us (3%)
    ppermute x27, starting transfers between devices, shift(): return lax.ppermute(v, axis, [(i, (i + k) % n) for i in range(n)])  40 us
    ppermute x27, waiting for transfers between devices, shift(): return lax.ppermute(v, axis, [(i, (i + k) % n) for i in range(n)])  38.1 us
    all_to_all x5, starting transfers between devices, exchange(): return lax.all_to_all(v, axis, 0, 0, tiled=True)  25.8 us
    pallas_call x1, Pallas kernels, decode(): pl.pallas_call(functools.partial(decode_kernel, width), in_specs=[pl.Bloc...  25.3 us
    all_to_all x5, waiting for transfers between devices, exchange(): return lax.all_to_all(v, axis, 0, 0, tiled=True)  23.6 us
    unnamed x39, local copies, waits for them, and re-layouts  5.93 us
    pallas_call x2, Pallas kernels, core_rows(): pl.pallas_call(functools.partial(core_rows_kernel, bool(got)), in_specs=[...  5 us
  transfers between devices with their start and end apart: 32, of which 16 were waited for; matrix products, arithmetic and copies ran while one was open for 6% of the time, Pallas kernels for 0%

profile of v3, /device:TPU:1, one launch (start us, length us, event | category | flops | bytes accessed | tf_op | source)
XLA Modules:
  0.0 179.7 jit_solution(18032637652541062815)
XLA Ops:
  0.6 2.3 %shard_map.146 = bf16[4,8,32,512]{3,2,1,0:T(8,128)(2,1)} custom-call(s32[1]{0:T(128)} %bitcast.2.core, f32[8,4,2,32,512]{4,3,2,1,0:T(8,128)} %bitcast.50), custom_call_target="tpu_custom_call" | custom-call | tf_op jit(solution)/shard_map/pallas_call | solution.py:69
  3.0 3.3 %collective-permute-start = (bf16[4,8,32,512]{3,2,1,0:T(8,128)(2,1)}, bf16[4,8,32,512]{3,2,1,0:T(8,128)(2,1)S(1)}, u32[]{:S(2)}, u32[]{:S(2)}) collective-permute-start(bf16[4,8,32,512]{3,2,1,0:T(8,128)(2,1)} %shard_map.146), channel_id=1, source_target_pairs={{0,4},{4,0},{1,5},{5,1},{2,6},{6,2},{3,7},{7,3},{8,12},{12,8},{9,1... | collective-permute-start | bytes 3145736 | tf_op jit(solution)/shard_map/ppermute | solution.py:34
  9.8 2.7 %shard_map.147 = bf16[4,8,32,512]{3,2,1,0:T(8,128)(2,1)} custom-call(s32[1]{0:T(128)} %bitcast.core, f32[8,4,2,32,512]{4,3,2,1,0:T(8,128)} %bitcast.51, bf16[4,8,32,512]{3,2,1,0:T(8,128)(2,1)} %copy-done.2), custom_call_target="tpu_custom_call" | custom-call | tf_op jit(solution)/shard_map/pallas_call | solution.py:69
  12.5 3.7 %all-to-all-start = ((bf16[4,8,32,512]{3,2,1,0:T(8,128)(2,1)}), bf16[4,8,32,512]{3,2,1,0:T(8,128)(2,1)S(1)}, u32[]{:S(2)}, u32[]{:S(2)}) async-start(bf16[4,8,32,512]{3,2,1,0:T(8,128)(2,1)} %shard_map.147), calls=%async_computation | async-start | bytes 2097152 | tf_op jit(solution)/shard_map/all_to_all | solution.py:28
  16.3 1.6 collective-permute-start.1
  19.1 5.1 %collective-permute-done.1.refs_1_ = bf16[64,2048]{1,0:T(8,128)(2,1)} collective-permute-done((bf16[64,2048]{1,0:T(8,128)(2,1)}, bf16[64,2048]{1,0:T(8,128)(2,1)}, u32[]{:S(2)}, u32[]{:S(2)}) %collective-permute-start.1) | collective-permute-done | bytes 262176 | tf_op jit(solution)/shard_map/ppermute | solution.py:34
  24.2 2.4 %collective-permute-done.2.refs_2_ = bf16[64,2048]{1,0:T(8,128)(2,1)} collective-permute-done((bf16[64,2048]{1,0:T(8,128)(2,1)}, bf16[64,2048]{1,0:T(8,128)(2,1)}, u32[]{:S(2)}, u32[]{:S(2)}) %collective-permute-start.2) | collective-permute-done | bytes 262176 | tf_op jit(solution)/shard_map/ppermute | solution.py:34
  26.6 6.9 %collective-permute-done.3.refs_3_ = bf16[64,2048]{1,0:T(8,128)(2,1)} collective-permute-done((bf16[64,2048]{1,0:T(8,128)(2,1)}, bf16[64,2048]{1,0:T(8,128)(2,1)}, u32[]{:S(2)}, u32[]{:S(2)}) %collective-permute-start.3) | collective-permute-done | bytes 262176 | tf_op jit(solution)/shard_map/ppermute | solution.py:34
  34.5 8.2 %all-to-all-start.1 = ((bf16[8,32,512]{2,1,0:T(8,128)(2,1)}), bf16[8,32,512]{2,1,0:T(8,128)(2,1)S(1)}, u32[]{:S(2)}, u32[]{:S(2)}) async-start(bf16[8,32,512]{2,1,0:T(8,128)(2,1)} %reduce_sum.30), calls=%async_computation.1 | async-start | bytes 524288 | tf_op jit(solution)/shard_map/all_to_all | solution.py:28
  44.0 2.7 %collective-permute-start.6 = (bf16[48,2176]{1,0:T(8,128)(2,1)}, bf16[48,2176]{1,0:T(8,128)(2,1)}, u32[]{:S(2)}, u32[]{:S(2)}) collective-permute-start(bf16[48,2176]{1,0:T(8,128)(2,1)} %get-tuple-element.65), channel_id=1, source_target_pairs={{0,24},{8,0},{16,8},{24,16},{1,25},{9,1},{17,9},{25,17},{2,26},{10... | collective-permute-start | bytes 626696 | tf_op jit(solution)/shard_map/ppermute | solution.py:34
  48.1 5.3 %all-to-all-done.1 = bf16[8,32,512]{2,1,0:T(8,128)(2,1)S(1)} async-done(((bf16[8,32,512]{2,1,0:T(8,128)(2,1)}), bf16[8,32,512]{2,1,0:T(8,128)(2,1)S(1)}, u32[]{:S(2)}, u32[]{:S(2)}) %all-to-all-start.1) | async-done | bytes 262176 | tf_op jit(solution)/shard_map/all_to_all | solution.py:28
  53.4 1.5 fusion.75
  55.7 3.4 %all-to-all-start.2 = ((bf16[8,32,512]{2,1,0:T(8,128)(2,1)}), bf16[8,32,512]{2,1,0:T(8,128)(2,1)S(1)}, u32[]{:S(2)}, u32[]{:S(2)}) async-start(bf16[8,32,512]{2,1,0:T(8,128)(2,1)} %broadcast_in_dim.14), calls=%async_computation.2 | async-start | bytes 524288 | tf_op jit(solution)/shard_map/all_to_all | solution.py:28
  60.0 2.7 %convolution_convert_fusion = bf16[256,2176]{1,0:T(8,128)(2,1)} fusion(bf16[48,2176]{1,0:T(8,128)(2,1)} %collective-permute-done.6, bf16[48,2176]{1,0:T(8,128)(2,1)} %collective-permute-done.5, bf16[48,2176]{1,0:T(8,128)(2,1)} %collective-permute-done.4, bf16[48,2176]{1,0:T(8,128)(2,1)S(1)} %get-tuple-element.64, s32[256]{0:T(256)S(1)} %compare_select_fusion.4), kind=kOutput, calls=%fused_computation.2 | convolution fusion | flops 217858048 | bytes 1950720 | tf_op jit(solution)/shard_map/dot_general | solution.py:255
  62.6 5.7 %all-to-all-done.2 = bf16[8,32,512]{2,1,0:T(8,128)(2,1)S(1)} async-done(((bf16[8,32,512]{2,1,0:T(8,128)(2,1)}), bf16[8,32,512]{2,1,0:T(8,128)(2,1)S(1)}, u32[]{:S(2)}, u32[]{:S(2)}) %all-to-all-start.2) | async-done | bytes 262176 | tf_op jit(solution)/shard_map/all_to_all | solution.py:28
  68.3 7.0 %all-to-all-start.3 = ((bf16[16,16,2176]{2,1,0:T(8,128)(2,1)}), bf16[16,16,2176]{2,1,0:T(8,128)(2,1)S(1)}, u32[]{:S(2)}, u32[]{:S(2)}) async-start(bf16[16,16,2176]{2,1,0:T(8,128)(2,1)} %bitcast.10), calls=%async_computation.3 | async-start | bytes 2228224 | tf_op jit(solution)/shard_map/all_to_all | solution.py:28
  75.4 2.8 %collective-permute-start.9 = (bf16[8,32,256]{2,1,0:T(8,128)(2,1)S(1)}, bf16[8,32,256]{2,1,0:T(8,128)(2,1)S(1)}, u32[]{:S(2)}, u32[]{:S(2)}) collective-permute-start(bf16[8,32,256]{2,1,0:T(8,128)(2,1)S(1)} %get-tuple-element.71), channel_id=1, source_target_pairs={{0,24},{8,0},{16,8},{24,16},{1,25},{9,1},{17,9},{25,17},{2,26},{10... | collective-permute-start | bytes 393224 | tf_op jit(solution)/shard_map/ppermute | solution.py:34
  79.6 3.8 %collective-permute-done.9 = bf16[8,32,256]{2,1,0:T(8,128)(2,1)S(1)} collective-permute-done((bf16[8,32,256]{2,1,0:T(8,128)(2,1)S(1)}, bf16[8,32,256]{2,1,0:T(8,128)(2,1)S(1)}, u32[]{:S(2)}, u32[]{:S(2)}) %collective-permute-start.9) | collective-permute-done | bytes 131104 | tf_op jit(solution)/shard_map/ppermute | solution.py:34
  84.2 3.7 %collective-permute-done.7 = bf16[8,32,256]{2,1,0:T(8,128)(2,1)S(1)} collective-permute-done((bf16[8,32,256]{2,1,0:T(8,128)(2,1)S(1)}, bf16[8,32,256]{2,1,0:T(8,128)(2,1)S(1)}, u32[]{:S(2)}, u32[]{:S(2)}) %collective-permute-start.7) | collective-permute-done | bytes 131104 | tf_op jit(solution)/shard_map/ppermute | solution.py:34
  89.7 1.9 %collective-permute-start.15 = (bf16[4,8,32,256]{3,2,1,0:T(8,128)(2,1)S(1)}, bf16[4,8,32,256]{3,2,1,0:T(8,128)(2,1)}, u32[]{:S(2)}, u32[]{:S(2)}) collective-permute-start(bf16[4,8,32,256]{3,2,1,0:T(8,128)(2,1)S(1)} %pad_maximum_fusion.refs_4_), channel_id=1, source_target_pairs={{0,3},{1,0},{2,1},{3,2},{4,7},{5,4},{6,5},{7,6},{8,11},{9,8},{10,9... | collective-permute-start | bytes 1572872 | tf_op jit(solution)/shard_map/ppermute | solution.py:34
  92.9 3.5 %collective-permute-start.17 = (bf16[4,8,32,256]{3,2,1,0:T(8,128)(2,1)S(1)}, bf16[4,8,32,256]{3,2,1,0:T(8,128)(2,1)}, u32[]{:S(2)}, u32[]{:S(2)}) collective-permute-start(bf16[4,8,32,256]{3,2,1,0:T(8,128)(2,1)S(1)} %pad_maximum_fusion.1.refs_12_), channel_id=1, source_target_pairs={{0,16},{8,24},{16,0},{24,8},{1,17},{9,25},{17,1},{25,9},{2,18},{10... | collective-permute-start | bytes 1572872 | tf_op jit(solution)/shard_map/ppermute | solution.py:34
  96.4 7.1 %collective-permute-done.13.refs_6_ = bf16[4,8,32,256]{3,2,1,0:T(8,128)(2,1)S(1)} collective-permute-done((bf16[4,8,32,256]{3,2,1,0:T(8,128)(2,1)S(1)}, bf16[4,8,32,256]{3,2,1,0:T(8,128)(2,1)S(1)}, u32[]{:S(2)}, u32[]{:S(2)}) %collective-permute-start.13) | collective-permute-done | bytes 524320 | tf_op jit(solution)/shard_map/ppermute | solution.py:34
  103.5 4.1 %collective-permute-start.18 = (bf16[4,8,32,256]{3,2,1,0:T(8,128)(2,1)S(1)}, bf16[4,8,32,256]{3,2,1,0:T(8,128)(2,1)}, u32[]{:S(2)}, u32[]{:S(2)}) collective-permute-start(bf16[4,8,32,256]{3,2,1,0:T(8,128)(2,1)S(1)} %pad_maximum_fusion.1.refs_12_), channel_id=1, source_target_pairs={{0,24},{8,0},{16,8},{24,16},{1,25},{9,1},{17,9},{25,17},{2,26},{10... | collective-permute-start | bytes 1572872 | tf_op jit(solution)/shard_map/ppermute | solution.py:34
  107.6 1.4 convolution_convert_fusion.1.slots_ref
  108.9 2.1 %collective-permute-done.14.refs_8_ = bf16[4,8,32,256]{3,2,1,0:T(8,128)(2,1)S(1)} collective-permute-done((bf16[4,8,32,256]{3,2,1,0:T(8,128)(2,1)S(1)}, bf16[4,8,32,256]{3,2,1,0:T(8,128)(2,1)S(1)}, u32[]{:S(2)}, u32[]{:S(2)}) %collective-permute-start.14) | collective-permute-done | bytes 524320 | tf_op jit(solution)/shard_map/ppermute | solution.py:34
  111.0 10.0 %collective-permute-start.19 = (bf16[4,8,32,256]{3,2,1,0:T(8,128)(2,1)S(1)}, bf16[4,8,32,256]{3,2,1,0:T(8,128)(2,1)S(1)}, u32[]{:S(2)}, u32[]{:S(2)}) collective-permute-start(bf16[4,8,32,256]{3,2,1,0:T(8,128)(2,1)S(1)} %pad_maximum_fusion.refs_4_), channel_id=1, source_target_pairs={{0,4},{4,0},{1,5},{5,1},{2,6},{6,2},{3,7},{7,3},{8,12},{12,8},{9,1... | collective-permute-start | bytes 1572872 | tf_op jit(solution)/shard_map/ppermute | solution.py:34
  121.1 4.1 %collective-permute-done.18.refs_18_ = bf16[4,8,32,256]{3,2,1,0:T(8,128)(2,1)} collective-permute-done((bf16[4,8,32,256]{3,2,1,0:T(8,128)(2,1)S(1)}, bf16[4,8,32,256]{3,2,1,0:T(8,128)(2,1)}, u32[]{:S(2)}, u32[]{:S(2)}) %collective-permute-start.18) | collective-permute-done | bytes 524320 | tf_op jit(solution)/shard_map/ppermute | solution.py:34
  125.2 2.9 %collective-permute-start.20 = (bf16[4,8,32,256]{3,2,1,0:T(8,128)(2,1)S(1)}, bf16[4,8,32,256]{3,2,1,0:T(8,128)(2,1)S(1)}, u32[]{:S(2)}, u32[]{:S(2)}) collective-permute-start(bf16[4,8,32,256]{3,2,1,0:T(8,128)(2,1)S(1)} %collective-permute-done.13.refs_6_), channel_id=1, source_target_pairs={{0,4},{4,0},{1,5},{5,1},{2,6},{6,2},{3,7},{7,3},{8,12},{12,8},{9,1... | collective-permute-start | bytes 1572872 | tf_op jit(solution)/shard_map/ppermute | solution.py:34
  135.4 25.3 %shard_map.148 = bf16[4,208,512]{2,1,0:T(8,128)(2,1)} custom-call(s32[4]{0:T(128)} %pad_add_fusion.place, bf16[192,2176]{1,0:T(8,128)(2,1)} %convolution_convert_fusion.1.slots_ref, bf16[128,2176]{1,0:T(8,128)(2,1)} %constant_dynamic-slice_fusion.envs_ref, bf16[256,2048]{1,0:T(8,128)(2,1)} %table_ref.1, f32[1,2048]{1,0:T(1,128)} %bitcast.68, ...), custom_call_target="tpu_custom_call" | custom-call | flops 10737418240 | bytes 8388608 | tf_op jit(solution)/shard_map/pallas_call | solution.py:175
  160.7 3.5 %all-to-all-start.4 = ((bf16[4,208,512]{2,1,0:T(8,128)(2,1)}), bf16[4,208,512]{2,1,0:T(8,128)(2,1)S(1)}, u32[]{:S(2)}, u32[]{:S(2)}) async-start(bf16[4,208,512]{2,1,0:T(8,128)(2,1)} %shard_map.148), calls=%async_computation.4 | async-start | bytes 1703936 | tf_op jit(solution)/shard_map/all_to_all | solution.py:28
  164.3 12.7 %all-to-all-done.4 = bf16[4,208,512]{2,1,0:T(8,128)(2,1)S(1)} async-done(((bf16[4,208,512]{2,1,0:T(8,128)(2,1)}), bf16[4,208,512]{2,1,0:T(8,128)(2,1)S(1)}, u32[]{:S(2)}, u32[]{:S(2)}) %all-to-all-start.4) | async-done | bytes 852000 | tf_op jit(solution)/shard_map/all_to_all | solution.py:28
  178.0 1.7 fusion.3
  (107 shorter events, 23.2 us)
Async XLA Ops:
  3.0 5.8 %collective-permute-start = (bf16[4,8,32,512]{3,2,1,0:T(8,128)(2,1)}, bf16[4,8,32,512]{3,2,1,0:T(8,128)(2,1)S(1)}, u32[]{:S(2)}, u32[]{:S(2)}) collective-permute-start(bf16[4,8,32,512]{3,2,1,0:T(8,128)(2,1)} %shard_map.146), channel_id=1, source_target_pairs={{0,4},{4,0},{1,5},{5,1},{2,6},{6,2},{3,7},{7,3},{8,12},{12,8},{9,1... | collective-permute-start | bytes 3145736 | tf_op jit(solution)/shard_map/ppermute | solution.py:34
  12.5 21.0 %all-to-all-start = ((bf16[4,8,32,512]{3,2,1,0:T(8,128)(2,1)}), bf16[4,8,32,512]{3,2,1,0:T(8,128)(2,1)S(1)}, u32[]{:S(2)}, u32[]{:S(2)}) async-start(bf16[4,8,32,512]{3,2,1,0:T(8,128)(2,1)} %shard_map.147), calls=%async_computation | async-start | bytes 2097152 | tf_op jit(solution)/shard_map/all_to_all | solution.py:28
  16.3 7.9 %collective-permute-start.1 = (bf16[64,2048]{1,0:T(8,128)(2,1)}, bf16[64,2048]{1,0:T(8,128)(2,1)}, u32[]{:S(2)}, u32[]{:S(2)}) collective-permute-start(bf16[64,2048]{1,0:T(8,128)(2,1)} %bitcast.64), channel_id=1, source_target_pairs={{0,3},{1,0},{2,1},{3,2},{4,7},{5,4},{6,5},{7,6},{8,11},{9,8},{10,9... | collective-permute-start | bytes 786440 | tf_op jit(solution)/shard_map/ppermute | solution.py:34
  17.9 8.7 %collective-permute-start.2 = (bf16[64,2048]{1,0:T(8,128)(2,1)}, bf16[64,2048]{1,0:T(8,128)(2,1)}, u32[]{:S(2)}, u32[]{:S(2)}) collective-permute-start(bf16[64,2048]{1,0:T(8,128)(2,1)} %bitcast.65), channel_id=1, source_target_pairs={{0,2},{1,3},{2,0},{3,1},{4,6},{5,7},{6,4},{7,5},{8,10},{9,11},{10,... | collective-permute-start | bytes 786440 | tf_op jit(solution)/shard_map/ppermute | solution.py:34
  18.2 15.3 %collective-permute-start.3 = (bf16[64,2048]{1,0:T(8,128)(2,1)}, bf16[64,2048]{1,0:T(8,128)(2,1)}, u32[]{:S(2)}, u32[]{:S(2)}) collective-permute-start(bf16[64,2048]{1,0:T(8,128)(2,1)} %bitcast.66), channel_id=1, source_target_pairs={{0,1},{1,2},{2,3},{3,0},{4,5},{5,6},{6,7},{7,4},{8,9},{9,10},{10,1... | collective-permute-start | bytes 786440 | tf_op jit(solution)/shard_map/ppermute | solution.py:34
  34.5 18.9 %all-to-all-start.1 = ((bf16[8,32,512]{2,1,0:T(8,128)(2,1)}), bf16[8,32,512]{2,1,0:T(8,128)(2,1)S(1)}, u32[]{:S(2)}, u32[]{:S(2)}) async-start(bf16[8,32,512]{2,1,0:T(8,128)(2,1)} %reduce_sum.30), calls=%async_computation.1 | async-start | bytes 524288 | tf_op jit(solution)/shard_map/all_to_all | solution.py:28
  44.0 15.9 %collective-permute-start.6 = (bf16[48,2176]{1,0:T(8,128)(2,1)}, bf16[48,2176]{1,0:T(8,128)(2,1)}, u32[]{:S(2)}, u32[]{:S(2)}) collective-permute-start(bf16[48,2176]{1,0:T(8,128)(2,1)} %get-tuple-element.65), channel_id=1, source_target_pairs={{0,24},{8,0},{16,8},{24,16},{1,25},{9,1},{17,9},{25,17},{2,26},{10... | collective-permute-start | bytes 626696 | tf_op jit(solution)/shard_map/ppermute | solution.py:34
  46.7 13.2 %collective-permute-start.5 = (bf16[48,2176]{1,0:T(8,128)(2,1)S(1)}, bf16[48,2176]{1,0:T(8,128)(2,1)}, u32[]{:S(2)}, u32[]{:S(2)}) collective-permute-start(bf16[48,2176]{1,0:T(8,128)(2,1)S(1)} %get-tuple-element.66), channel_id=1, source_target_pairs={{0,16},{8,24},{16,0},{24,8},{1,17},{9,25},{17,1},{25,9},{2,18},{10... | collective-permute-start | bytes 626696 | tf_op jit(solution)/shard_map/ppermute | solution.py:34
  47.3 12.6 %collective-permute-start.4 = (bf16[48,2176]{1,0:T(8,128)(2,1)S(1)}, bf16[48,2176]{1,0:T(8,128)(2,1)}, u32[]{:S(2)}, u32[]{:S(2)}) collective-permute-start(bf16[48,2176]{1,0:T(8,128)(2,1)S(1)} %get-tuple-element.67), channel_id=1, source_target_pairs={{0,8},{8,16},{16,24},{24,0},{1,9},{9,17},{17,25},{25,1},{2,10},{10... | collective-permute-start | bytes 626696 | tf_op jit(solution)/shard_map/ppermute | solution.py:34
  55.7 12.6 %all-to-all-start.2 = ((bf16[8,32,512]{2,1,0:T(8,128)(2,1)}), bf16[8,32,512]{2,1,0:T(8,128)(2,1)S(1)}, u32[]{:S(2)}, u32[]{:S(2)}) async-start(bf16[8,32,512]{2,1,0:T(8,128)(2,1)} %broadcast_in_dim.14), calls=%async_computation.2 | async-start | bytes 524288 | tf_op jit(solution)/shard_map/all_to_all | solution.py:28
  68.3 39.3 %all-to-all-start.3 = ((bf16[16,16,2176]{2,1,0:T(8,128)(2,1)}), bf16[16,16,2176]{2,1,0:T(8,128)(2,1)S(1)}, u32[]{:S(2)}, u32[]{:S(2)}) async-start(bf16[16,16,2176]{2,1,0:T(8,128)(2,1)} %bitcast.10), calls=%async_computation.3 | async-start | bytes 2228224 | tf_op jit(solution)/shard_map/all_to_all | solution.py:28
  75.4 8.1 %collective-permute-start.9 = (bf16[8,32,256]{2,1,0:T(8,128)(2,1)S(1)}, bf16[8,32,256]{2,1,0:T(8,128)(2,1)S(1)}, u32[]{:S(2)}, u32[]{:S(2)}) collective-permute-start(bf16[8,32,256]{2,1,0:T(8,128)(2,1)S(1)} %get-tuple-element.71), channel_id=1, source_target_pairs={{0,24},{8,0},{16,8},{24,16},{1,25},{9,1},{17,9},{25,17},{2,26},{10... | collective-permute-start | bytes 393224 | tf_op jit(solution)/shard_map/ppermute | solution.py:34
  78.1 6.1 %collective-permute-start.8 = (bf16[8,32,256]{2,1,0:T(8,128)(2,1)S(1)}, bf16[8,32,256]{2,1,0:T(8,128)(2,1)S(1)}, u32[]{:S(2)}, u32[]{:S(2)}) collective-permute-start(bf16[8,32,256]{2,1,0:T(8,128)(2,1)S(1)} %get-tuple-element.71), channel_id=1, source_target_pairs={{0,16},{8,24},{16,0},{24,8},{1,17},{9,25},{17,1},{25,9},{2,18},{10... | collective-permute-start | bytes 393224 | tf_op jit(solution)/shard_map/ppermute | solution.py:34
  78.7 9.2 %collective-permute-start.7 = (bf16[8,32,256]{2,1,0:T(8,128)(2,1)S(1)}, bf16[8,32,256]{2,1,0:T(8,128)(2,1)S(1)}, u32[]{:S(2)}, u32[]{:S(2)}) collective-permute-start(bf16[8,32,256]{2,1,0:T(8,128)(2,1)S(1)} %get-tuple-element.71), channel_id=1, source_target_pairs={{0,8},{8,16},{16,24},{24,0},{1,9},{9,17},{17,25},{25,1},{2,10},{10... | collective-permute-start | bytes 393224 | tf_op jit(solution)/shard_map/ppermute | solution.py:34
  79.3 8.7 %collective-permute-start.12 = (bf16[8,32,256]{2,1,0:T(8,128)(2,1)S(1)}, bf16[8,32,256]{2,1,0:T(8,128)(2,1)S(1)}, u32[]{:S(2)}, u32[]{:S(2)}) collective-permute-start(bf16[8,32,256]{2,1,0:T(8,128)(2,1)S(1)} %get-tuple-element.70), channel_id=1, source_target_pairs={{0,3},{1,0},{2,1},{3,2},{4,7},{5,4},{6,5},{7,6},{8,11},{9,8},{10,9... | collective-permute-start | bytes 393224 | tf_op jit(solution)/shard_map/ppermute | solution.py:34
  79.3 8.7 %collective-permute-start.11 = (bf16[8,32,256]{2,1,0:T(8,128)(2,1)S(1)}, bf16[8,32,256]{2,1,0:T(8,128)(2,1)S(1)}, u32[]{:S(2)}, u32[]{:S(2)}) collective-permute-start(bf16[8,32,256]{2,1,0:T(8,128)(2,1)S(1)} %get-tuple-element.70), channel_id=1, source_target_pairs={{0,2},{1,3},{2,0},{3,1},{4,6},{5,7},{6,4},{7,5},{8,10},{9,11},{10,... | collective-permute-start | bytes 393224 | tf_op jit(solution)/shard_map/ppermute | solution.py:34
  83.5 5.3 %collective-permute-start.10 = (bf16[8,32,256]{2,1,0:T(8,128)(2,1)S(1)}, bf16[8,32,256]{2,1,0:T(8,128)(2,1)S(1)}, u32[]{:S(2)}, u32[]{:S(2)}) collective-permute-start(bf16[8,32,256]{2,1,0:T(8,128)(2,1)S(1)} %get-tuple-element.70), channel_id=1, source_target_pairs={{0,1},{1,2},{2,3},{3,0},{4,5},{5,6},{6,7},{7,4},{8,9},{9,10},{10,1... | collective-permute-start | bytes 393224 | tf_op jit(solution)/shard_map/ppermute | solution.py:34
  88.9 14.6 %collective-permute-start.13 = (bf16[4,8,32,256]{3,2,1,0:T(8,128)(2,1)S(1)}, bf16[4,8,32,256]{3,2,1,0:T(8,128)(2,1)S(1)}, u32[]{:S(2)}, u32[]{:S(2)}) collective-permute-start(bf16[4,8,32,256]{3,2,1,0:T(8,128)(2,1)S(1)} %pad_maximum_fusion.refs_4_), channel_id=1, source_target_pairs={{0,1},{1,2},{2,3},{3,0},{4,5},{5,6},{6,7},{7,4},{8,9},{9,10},{10,1... | collective-permute-start | bytes 1572872 | tf_op jit(solution)/shard_map/ppermute | solution.py:34
  89.0 22.0 %collective-permute-start.14 = (bf16[4,8,32,256]{3,2,1,0:T(8,128)(2,1)S(1)}, bf16[4,8,32,256]{3,2,1,0:T(8,128)(2,1)S(1)}, u32[]{:S(2)}, u32[]{:S(2)}) collective-permute-start(bf16[4,8,32,256]{3,2,1,0:T(8,128)(2,1)S(1)} %pad_maximum_fusion.refs_4_), channel_id=1, source_target_pairs={{0,2},{1,3},{2,0},{3,1},{4,6},{5,7},{6,4},{7,5},{8,10},{9,11},{10,... | collective-permute-start | bytes 1572872 | tf_op jit(solution)/shard_map/ppermute | solution.py:34
  89.7 31.2 %collective-permute-start.15 = (bf16[4,8,32,256]{3,2,1,0:T(8,128)(2,1)S(1)}, bf16[4,8,32,256]{3,2,1,0:T(8,128)(2,1)}, u32[]{:S(2)}, u32[]{:S(2)}) collective-permute-start(bf16[4,8,32,256]{3,2,1,0:T(8,128)(2,1)S(1)} %pad_maximum_fusion.refs_4_), channel_id=1, source_target_pairs={{0,3},{1,0},{2,1},{3,2},{4,7},{5,4},{6,5},{7,6},{8,11},{9,8},{10,9... | collective-permute-start | bytes 1572872 | tf_op jit(solution)/shard_map/ppermute | solution.py:34
  91.6 29.5 %collective-permute-start.16 = (bf16[4,8,32,256]{3,2,1,0:T(8,128)(2,1)S(1)}, bf16[4,8,32,256]{3,2,1,0:T(8,128)(2,1)}, u32[]{:S(2)}, u32[]{:S(2)}) collective-permute-start(bf16[4,8,32,256]{3,2,1,0:T(8,128)(2,1)S(1)} %pad_maximum_fusion.1.refs_12_), channel_id=1, source_target_pairs={{0,8},{8,16},{16,24},{24,0},{1,9},{9,17},{17,25},{25,1},{2,10},{10... | collective-permute-start | bytes 1572872 | tf_op jit(solution)/shard_map/ppermute | solution.py:34
  92.9 28.2 %collective-permute-start.17 = (bf16[4,8,32,256]{3,2,1,0:T(8,128)(2,1)S(1)}, bf16[4,8,32,256]{3,2,1,0:T(8,128)(2,1)}, u32[]{:S(2)}, u32[]{:S(2)}) collective-permute-start(bf16[4,8,32,256]{3,2,1,0:T(8,128)(2,1)S(1)} %pad_maximum_fusion.1.refs_12_), channel_id=1, source_target_pairs={{0,16},{8,24},{16,0},{24,8},{1,17},{9,25},{17,1},{25,9},{2,18},{10... | collective-permute-start | bytes 1572872 | tf_op jit(solution)/shard_map/ppermute | solution.py:34
  103.5 21.7 %collective-permute-start.18 = (bf16[4,8,32,256]{3,2,1,0:T(8,128)(2,1)S(1)}, bf16[4,8,32,256]{3,2,1,0:T(8,128)(2,1)}, u32[]{:S(2)}, u32[]{:S(2)}) collective-permute-start(bf16[4,8,32,256]{3,2,1,0:T(8,128)(2,1)S(1)} %pad_maximum_fusion.1.refs_12_), channel_id=1, source_target_pairs={{0,24},{8,0},{16,8},{24,16},{1,25},{9,1},{17,9},{25,17},{2,26},{10... | collective-permute-start | bytes 1572872 | tf_op jit(solution)/shard_map/ppermute | solution.py:34
  111.0 17.7 %collective-permute-start.19 = (bf16[4,8,32,256]{3,2,1,0:T(8,128)(2,1)S(1)}, bf16[4,8,32,256]{3,2,1,0:T(8,128)(2,1)S(1)}, u32[]{:S(2)}, u32[]{:S(2)}) collective-permute-start(bf16[4,8,32,256]{3,2,1,0:T(8,128)(2,1)S(1)} %pad_maximum_fusion.refs_4_), channel_id=1, source_target_pairs={{0,4},{4,0},{1,5},{5,1},{2,6},{6,2},{3,7},{7,3},{8,12},{12,8},{9,1... | collective-permute-start | bytes 1572872 | tf_op jit(solution)/shard_map/ppermute | solution.py:34
  121.0 7.8 %collective-permute-start.23 = (bf16[4,8,32,256]{3,2,1,0:T(8,128)(2,1)S(1)}, bf16[4,8,32,256]{3,2,1,0:T(8,128)(2,1)S(1)}, u32[]{:S(2)}, u32[]{:S(2)}) collective-permute-start(bf16[4,8,32,256]{3,2,1,0:T(8,128)(2,1)S(1)} %pad_maximum_fusion.1.refs_12_), channel_id=1, source_target_pairs={{0,4},{4,0},{1,5},{5,1},{2,6},{6,2},{3,7},{7,3},{8,12},{12,8},{9,1... | collective-permute-start | bytes 1572872 | tf_op jit(solution)/shard_map/ppermute | solution.py:34
  125.2 4.5 %collective-permute-start.20 = (bf16[4,8,32,256]{3,2,1,0:T(8,128)(2,1)S(1)}, bf16[4,8,32,256]{3,2,1,0:T(8,128)(2,1)S(1)}, u32[]{:S(2)}, u32[]{:S(2)}) collective-permute-start(bf16[4,8,32,256]{3,2,1,0:T(8,128)(2,1)S(1)} %collective-permute-done.13.refs_6_), channel_id=1, source_target_pairs={{0,4},{4,0},{1,5},{5,1},{2,6},{6,2},{3,7},{7,3},{8,12},{12,8},{9,1... | collective-permute-start | bytes 1572872 | tf_op jit(solution)/shard_map/ppermute | solution.py:34
  128.2 3.0 %collective-permute-start.21 = (bf16[4,8,32,256]{3,2,1,0:T(8,128)(2,1)S(1)}, bf16[4,8,32,256]{3,2,1,0:T(8,128)(2,1)S(1)}, u32[]{:S(2)}, u32[]{:S(2)}) collective-permute-start(bf16[4,8,32,256]{3,2,1,0:T(8,128)(2,1)S(1)} %collective-permute-done.14.refs_8_), channel_id=1, source_target_pairs={{0,4},{4,0},{1,5},{5,1},{2,6},{6,2},{3,7},{7,3},{8,12},{12,8},{9,1... | collective-permute-start | bytes 1572872 | tf_op jit(solution)/shard_map/ppermute | solution.py:34
  128.2 3.9 %collective-permute-start.22 = (bf16[4,8,32,256]{3,2,1,0:T(8,128)(2,1)}, bf16[4,8,32,256]{3,2,1,0:T(8,128)(2,1)S(1)}, u32[]{:S(2)}, u32[]{:S(2)}) collective-permute-start(bf16[4,8,32,256]{3,2,1,0:T(8,128)(2,1)} %collective-permute-done.15.refs_10_), channel_id=1, source_target_pairs={{0,4},{4,0},{1,5},{5,1},{2,6},{6,2},{3,7},{7,3},{8,12},{12,8},{9,1... | collective-permute-start | bytes 1572872 | tf_op jit(solution)/shard_map/ppermute | solution.py:34
  128.7 4.2 %collective-permute-start.24 = (bf16[4,8,32,256]{3,2,1,0:T(8,128)(2,1)}, bf16[4,8,32,256]{3,2,1,0:T(8,128)(2,1)S(1)}, u32[]{:S(2)}, u32[]{:S(2)}) collective-permute-start(bf16[4,8,32,256]{3,2,1,0:T(8,128)(2,1)} %collective-permute-done.16.refs_14_), channel_id=1, source_target_pairs={{0,4},{4,0},{1,5},{5,1},{2,6},{6,2},{3,7},{7,3},{8,12},{12,8},{9,1... | collective-permute-start | bytes 1572872 | tf_op jit(solution)/shard_map/ppermute | solution.py:34
  128.8 4.9 %collective-permute-start.25 = (bf16[4,8,32,256]{3,2,1,0:T(8,128)(2,1)}, bf16[4,8,32,256]{3,2,1,0:T(8,128)(2,1)S(1)}, u32[]{:S(2)}, u32[]{:S(2)}) collective-permute-start(bf16[4,8,32,256]{3,2,1,0:T(8,128)(2,1)} %collective-permute-done.17.refs_16_), channel_id=1, source_target_pairs={{0,4},{4,0},{1,5},{5,1},{2,6},{6,2},{3,7},{7,3},{8,12},{12,8},{9,1... | collective-permute-start | bytes 1572872 | tf_op jit(solution)/shard_map/ppermute | solution.py:34
  129.7 4.8 %collective-permute-start.26 = (bf16[4,8,32,256]{3,2,1,0:T(8,128)(2,1)}, bf16[4,8,32,256]{3,2,1,0:T(8,128)(2,1)S(1)}, u32[]{:S(2)}, u32[]{:S(2)}) collective-permute-start(bf16[4,8,32,256]{3,2,1,0:T(8,128)(2,1)} %collective-permute-done.18.refs_18_), channel_id=1, source_target_pairs={{0,4},{4,0},{1,5},{5,1},{2,6},{6,2},{3,7},{7,3},{8,12},{12,8},{9,1... | collective-permute-start | bytes 1572872 | tf_op jit(solution)/shard_map/ppermute | solution.py:34
  160.7 16.2 %all-to-all-start.4 = ((bf16[4,208,512]{2,1,0:T(8,128)(2,1)}), bf16[4,208,512]{2,1,0:T(8,128)(2,1)S(1)}, u32[]{:S(2)}, u32[]{:S(2)}) async-start(bf16[4,208,512]{2,1,0:T(8,128)(2,1)} %shard_map.148), calls=%async_computation.4 | async-start | bytes 1703936 | tf_op jit(solution)/shard_map/all_to_all | solution.py:28
  (19 other events, 232.1 us)
